TPU v7x, 32 devices: a whole 2x2x4 slice. The times are simulated.
32 devices in a mesh: section: 2 (over x), dp: 8 (over z, core), rep: 2 (over y).
Axes of the slice: x: 2, y: 2, z: 4, core: 2. Of those that a mesh axis runs over, the one named last changes fastest.
Arguments:
- tokens: bfloat16 [32, 1024, 512], P(('dp', 'rep')), may hold values from -6 to 6
- resets: int32 [32, 1024], P(('dp', 'rep')), may hold values 0 or 1
- cotangent: bfloat16 [32, 1024, 512], P(('dp', 'rep')), may hold values from -6 to 6
- g_one: float32 [2, 512], P('section'), may hold values from 0.25 to 1.75
- w_gate: bfloat16 [2, 512, 2048], P('section'), may hold values from -0.25 to 0.25
- b_gate: float32 [2, 2048], P('section'), may hold values from -8 to 8
- w_cand: bfloat16 [2, 512, 1024], P('section'), may hold values from -0.25 to 0.25
- b_cand: float32 [2, 1024], P('section'), may hold values from -3 to 3
- w_out: bfloat16 [2, 1024, 512], P('section'), may hold values from -0.1875 to 0.1875
- b_out: float32 [2, 512], P('section'), may hold values from -3 to 3
- g_two: float32 [2, 512], P('section'), may hold values from 0.25 to 1.75
- w_up: bfloat16 [2, 512, 2048], P('section'), may hold values from -0.25 to 0.25
- b_up: float32 [2, 2048], P('section'), may hold values from -3 to 3
- w_down: bfloat16 [2, 2048, 512], P('section'), may hold values from -0.125 to 0.125
- b_down: float32 [2, 512], P('section'), may hold values from -3 to 3
Outputs:
- block_outputs: bfloat16 [2, 32, 1024, 512], P('section', ('dp', 'rep'))
- input_grads: float32 [2, 32, 1024, 512], P('section', ('dp', 'rep'))
- grad_g_one: float32 [2, 512], P('section')
- grad_w_gate: float32 [2, 512, 2048], P('section')
- grad_b_gate: float32 [2, 2048], P('section')
- grad_w_cand: float32 [2, 512, 1024], P('section')
- grad_b_cand: float32 [2, 1024], P('section')
- grad_w_out: float32 [2, 1024, 512], P('section')
- grad_b_out: float32 [2, 512], P('section')
- grad_g_two: float32 [2, 512], P('section')
- grad_w_up: float32 [2, 512, 2048], P('section')
- grad_b_up: float32 [2, 2048], P('section')
- grad_w_down: float32 [2, 2048, 512], P('section')
- grad_b_down: float32 [2, 512], P('section')
All inputs are finite; a program needn't handle non-finite values. No bound on the sum of `resets` on one device may be relied on, other than what follows from the above.
Results may differ from a plain program's by a relative error of at most 0.013.
Values may be sent and summed in bfloat16 or wider, within the bound.
A program may use at most 320 MiB of HBM per device.

v0:
```python
import jax
import jax.numpy as jnp
from jax import lax
from jax.sharding import PartitionSpec as P

EPS = 1e-06


def shifted(x, axis, by):
    peers = lax.axis_size(axis)
    pairs = [(i, i + by) for i in range(peers) if 0 <= i + by < peers]
    return lax.ppermute(x, axis, pairs)


def matmul(operand, weight):
    return jnp.dot(operand, weight, preferred_element_type=jnp.float32)


def matmul_back(operand, weight):
    return lax.dot_general(
        operand, weight, (((1,), (1,)), ((), ())), preferred_element_type=jnp.float32
    )


def weight_grad(operand, gradient):
    return lax.dot_general(
        operand, gradient, (((0,), (0,)), ((), ())), preferred_element_type=jnp.float32
    )


def inv_scale(values):
    return lax.rsqrt(jnp.mean(values * values, axis=-1, keepdims=True) + EPS)


def rms_back(values, inv_norm, norm_gain, grad_normed):
    weighted = grad_normed * norm_gain
    grad_gain = jnp.sum(grad_normed * values * inv_norm, axis=0)
    grad_values = inv_norm * weighted - values * inv_norm**3 * jnp.mean(
        weighted * values, axis=-1, keepdims=True
    )
    return (grad_values, grad_gain)


def block_scan(coeff, drive, reverse):
    seq_len, width = coeff.shape
    span = min(32, seq_len)
    groups = seq_len // span
    coeff_t = coeff.reshape((groups, span, width)).transpose((1, 0, 2))
    drive_t = drive.reshape((groups, span, width)).transpose((1, 0, 2))
    order = list(range(span))
    if reverse:
        order = order[::-1]
    product = jnp.ones((groups, width), jnp.float32)
    accum = jnp.zeros((groups, width), jnp.float32)
    inc_prod = [None] * span
    inc_acc = [None] * span
    exc_prod = [None] * span
    exc_acc = [None] * span
    for position in order:
        exc_prod[position] = product
        exc_acc[position] = accum
        accum = coeff_t[position] * accum + drive_t[position]
        product = coeff_t[position] * product
        inc_prod[position] = product
        inc_acc[position] = accum
    group_order = list(range(groups))
    if reverse:
        group_order = group_order[::-1]
    carry_val = jnp.zeros((width,), jnp.float32)
    incoming = [None] * groups
    for group_idx in group_order:
        incoming[group_idx] = carry_val
        carry_val = product[group_idx] * carry_val + accum[group_idx]
    carry_in = jnp.stack(incoming)[None]
    inclusive = jnp.stack(inc_acc) + jnp.stack(inc_prod) * carry_in
    exclusive = jnp.stack(exc_acc) + jnp.stack(exc_prod) * carry_in
    inclusive = inclusive.transpose((1, 0, 2)).reshape((seq_len, width))
    exclusive = exclusive.transpose((1, 0, 2)).reshape((seq_len, width))
    return (inclusive, exclusive)


def forward(resid_in, keep_mask, weights):
    g_one, w_gate, b_gate, w_cand, b_cand, w_out, b_out, g_two, w_up, b_up, w_down, b_down = weights
    hidden_width = w_cand.shape[1]
    inv_one = inv_scale(resid_in)
    normed = (resid_in * inv_one * g_one).astype(jnp.bfloat16)
    gate_pre = matmul(normed, w_gate) + b_gate
    forget = jax.nn.sigmoid(gate_pre[:, :hidden_width])
    inward = jax.nn.sigmoid(gate_pre[:, hidden_width:])
    gate_total = forget + inward
    candidate = matmul(normed, w_cand) + b_cand
    decay_rate = forget / gate_total * keep_mask[:, None]
    drive_term = inward / gate_total * candidate
    hidden_state, previous = block_scan(decay_rate, drive_term, False)
    state_low = hidden_state.astype(jnp.bfloat16)
    middle = resid_in + (matmul(state_low, w_out) + b_out)
    inv_two = inv_scale(middle)
    normed_two = (middle * inv_two * g_two).astype(jnp.bfloat16)
    up_pre = matmul(normed_two, w_up) + b_up
    active = jax.nn.gelu(up_pre, approximate=True).astype(jnp.bfloat16)
    result = middle + (matmul(active, w_down) + b_down)
    saved_vals = (
        resid_in,
        inv_one,
        normed,
        forget,
        inward,
        gate_total,
        candidate,
        decay_rate,
        previous,
        state_low,
        middle,
        inv_two,
        normed_two,
        up_pre,
        active,
    )
    return (result, saved_vals)


def backward(saved_vals, keep_mask, weights, grad_out):
    g_one, w_gate, b_gate, w_cand, b_cand, w_out, b_out, g_two, w_up, b_up, w_down, b_down = weights
    (
        resid_in,
        inv_one,
        normed,
        forget,
        inward,
        gate_total,
        candidate,
        decay_rate,
        previous,
        state_low,
        middle,
        inv_two,
        normed_two,
        up_pre,
        active,
    ) = saved_vals
    grad_down = grad_out.astype(jnp.bfloat16)
    grad_w_down = weight_grad(active, grad_down)
    grad_b_down = jnp.sum(grad_down.astype(jnp.float32), axis=0)
    grad_active = matmul_back(grad_down, w_down)
    _, gelu_back = jax.vjp(lambda value: jax.nn.gelu(value, approximate=True), up_pre)
    grad_up = gelu_back(grad_active)[0].astype(jnp.bfloat16)
    grad_w_up = weight_grad(normed_two, grad_up)
    grad_b_up = jnp.sum(grad_up.astype(jnp.float32), axis=0)
    grad_norm_two = matmul_back(grad_up, w_up)
    grad_middle_norm, grad_g_two = rms_back(middle, inv_two, g_two, grad_norm_two)
    grad_middle = grad_out + grad_middle_norm
    grad_mix = grad_middle.astype(jnp.bfloat16)
    grad_w_out = weight_grad(state_low, grad_mix)
    grad_b_out = jnp.sum(grad_mix.astype(jnp.float32), axis=0)
    grad_state = matmul_back(grad_mix, w_out)
    _, later_part = block_scan(decay_rate, decay_rate * grad_state, True)
    carried = grad_state + later_part
    grad_candidate = (carried * (inward / gate_total)).astype(jnp.bfloat16)
    grad_in_share = carried * candidate
    grad_forget_share = carried * previous * keep_mask[:, None]
    square = gate_total * gate_total
    grad_forget = (grad_forget_share - grad_in_share) * inward / square
    grad_inward = (grad_in_share - grad_forget_share) * forget / square
    grad_gate = jnp.concatenate(
        [grad_forget * forget * (1.0 - forget), grad_inward * inward * (1.0 - inward)], axis=1
    ).astype(jnp.bfloat16)
    grad_w_gate = weight_grad(normed, grad_gate)
    grad_b_gate = jnp.sum(grad_gate.astype(jnp.float32), axis=0)
    grad_w_cand = weight_grad(normed, grad_candidate)
    grad_b_cand = jnp.sum(grad_candidate.astype(jnp.float32), axis=0)
    grad_normed = matmul_back(grad_gate, w_gate) + matmul_back(grad_candidate, w_cand)
    grad_input_norm, grad_g_one = rms_back(resid_in, inv_one, g_one, grad_normed)
    grad_input = grad_middle + grad_input_norm
    return (
        grad_input,
        (
            grad_g_one,
            grad_w_gate,
            grad_b_gate,
            grad_w_cand,
            grad_b_cand,
            grad_w_out,
            grad_b_out,
            grad_g_two,
            grad_w_up,
            grad_b_up,
            grad_w_down,
            grad_b_down,
        ),
    )


def body(
    tokens,
    resets,
    cotangent,
    g_one,
    w_gate,
    b_gate,
    w_cand,
    b_cand,
    w_out,
    b_out,
    g_two,
    w_up,
    b_up,
    w_down,
    b_down,
):
    stacked = (
        g_one,
        w_gate,
        b_gate,
        w_cand,
        b_cand,
        w_out,
        b_out,
        g_two,
        w_up,
        b_up,
        w_down,
        b_down,
    )
    weights = tuple((member[0] for member in stacked))
    row_count = tokens.shape[0]
    section_index = lax.axis_index("section")
    is_first = section_index == 0
    keep_rows = (1 - resets).astype(jnp.float32)
    received = jnp.zeros(tokens.shape[1:], jnp.bfloat16)
    kept = []
    sent_rows = []
    for tick_step in range(row_count + 1):
        row_first = min(tick_step, row_count - 1)
        row_second = max(tick_step - 1, 0)
        resid_in = jnp.where(is_first, tokens[row_first], received).astype(jnp.float32)
        keep_mask = jnp.where(is_first, keep_rows[row_first], keep_rows[row_second])
        result, saved_vals = forward(resid_in, keep_mask, weights)
        low_result = result.astype(jnp.bfloat16)
        sent_rows.append(low_result)
        kept.append((saved_vals, keep_mask))
        if tick_step < row_count:
            received = shifted(low_result, "section", 1)
    block_rows = jnp.stack(
        [jnp.where(is_first, sent_rows[row], sent_rows[row + 1]) for row in range(row_count)]
    )
    returned = jnp.zeros(tokens.shape[1:], jnp.bfloat16)
    totals = None
    back_full = []
    back_low = []
    for tick_step in range(row_count + 1):
        source_tick = row_count - tick_step
        saved_vals, keep_mask = kept[source_tick]
        row_second = max(row_count - 1 - tick_step, 0)
        grad_out = jnp.where(is_first, returned, cotangent[row_second]).astype(jnp.float32)
        grad_input, grads = backward(saved_vals, keep_mask, weights, grad_out)
        valid_flag = jnp.where(
            is_first, 1.0 if tick_step >= 1 else 0.0, 1.0 if tick_step < row_count else 0.0
        )
        grads = tuple((member * valid_flag for member in grads))
        if totals is None:
            totals = grads
        else:
            totals = tuple((total_a + total_b for total_a, total_b in zip(totals, grads)))
        low_grad = grad_input.astype(jnp.bfloat16)
        back_full.append(grad_input)
        back_low.append(low_grad)
        if tick_step < row_count:
            returned = shifted(low_grad, "section", -1)
    grad_rows = jnp.stack(
        [
            jnp.where(
                is_first,
                back_full[row_count - row],
                back_low[row_count - 1 - row].astype(jnp.float32),
            )
            for row in range(row_count)
        ]
    )
    (
        sum_g_one,
        sum_w_gate,
        sum_b_gate,
        sum_w_cand,
        sum_b_cand,
        sum_w_out,
        sum_b_out,
        sum_g_two,
        sum_w_up,
        sum_b_up,
        sum_w_down,
        sum_b_down,
    ) = totals
    summed = lax.psum(
        (
            sum_g_one,
            sum_w_gate,
            sum_b_gate,
            sum_w_cand,
            sum_b_cand,
            sum_w_out,
            sum_b_out,
            sum_g_two,
            sum_w_up,
            sum_b_up,
            sum_w_down,
            sum_b_down,
        ),
        ("dp", "rep"),
    )
    outs_grads = tuple((member[None] for member in summed))
    return (block_rows[None], grad_rows[None]) + outs_grads


def solution(mesh):
    in_specs = (
        P(("dp", "rep"), None, None),
        P(("dp", "rep"), None),
        P(("dp", "rep"), None, None),
        P("section", None),
        P("section", None, None),
        P("section", None),
        P("section", None, None),
        P("section", None),
        P("section", None, None),
        P("section", None),
        P("section", None),
        P("section", None, None),
        P("section", None),
        P("section", None, None),
        P("section", None),
    )
    out_specs = (
        P("section", ("dp", "rep"), None, None),
        P("section", ("dp", "rep"), None, None),
        P("section", None),
        P("section", None, None),
        P("section", None),
        P("section", None, None),
        P("section", None),
        P("section", None, None),
        P("section", None),
        P("section", None),
        P("section", None, None),
        P("section", None),
        P("section", None, None),
        P("section", None),
    )
    return jax.shard_map(body, mesh=mesh, in_specs=in_specs, out_specs=out_specs, check_vma=False)
```

profile of v0, /device:TPU:0, one launch (start us, length us, event | category | flops | bytes accessed | tf_op | source)
XLA Modules:
  0.0 989.0 jit_solution(10554100139698259138)
XLA Ops:
  11.5 4.5 broadcast_add_fusion.2
  16.1 6.2 divide_multiply_fusion.2
  79.3 10.7 %add_bitcast_fusion.3 = (f32[32,32,1024]{2,0,1:T(8,128)}, bf16[32,32,1024]{2,0,1:T(8,128)(2,1)S(1)}) fusion(f32[32,32,1024]{2,1,0:T(8,128)} %copy-done.84, f32[32,32,1024]{2,1,0:T(8,128)} %copy-done.88, f32[32,1024]{1,0:T(8,128)S(1)} %stack.62, f32[32,32,1024]{2,1,0:T(8,128)} %copy-done.92, f32[32,32,1024]{2,1,0:T(8,128)} %copy-done.91), kind=kLoop, calls=%fused_computation.97 | loop fusion | flops 5242880 | bytes 23199744 | tf_op jit(solution)/shard_map/transpose | solution.py:78
  96.5 3.4 add_convert_fusion.5
  100.0 4.9 collective-permute-start
  105.0 22.3 %collective-permute-done = bf16[1024,512]{1,0:T(8,128)(2,1)S(1)} collective-permute-done((bf16[1024,512]{1,0:T(8,128)(2,1)S(1)}, bf16[1024,512]{1,0:T(8,128)(2,1)S(1)}, u32[]{:S(2)}, u32[]{:S(2)}) %collective-permute-start) | collective-permute-done | bytes 1048608 | tf_op jit(solution)/shard_map/ppermute | solution.py:12
  130.9 6.3 divide_multiply_fusion.1
  193.4 10.6 %add_bitcast_fusion.5 = (f32[32,32,1024]{2,0,1:T(8,128)}, bf16[32,32,1024]{2,0,1:T(8,128)(2,1)S(1)}) fusion(f32[32,32,1024]{2,1,0:T(8,128)} %copy-done.86, f32[32,32,1024]{2,1,0:T(8,128)} %copy-done.90, f32[32,1024]{1,0:T(8,128)S(1)} %stack.65, f32[32,32,1024]{2,1,0:T(8,128)} %copy-done.94, f32[32,32,1024]{2,1,0:T(8,128)} %copy-done.93), kind=kLoop, calls=%fused_computation.102 | loop fusion | flops 5242880 | bytes 23199744 | tf_op jit(solution)/shard_map/transpose | solution.py:78
  207.4 6.6 multiply_convert_fusion.1
  216.3 5.4 collective-permute-start.1
  221.7 6.8 copy.178
  230.7 4.4 copy.175
  236.1 6.2 collective-permute-done.1
  245.7 6.3 divide_multiply_fusion
  309.3 9.4 add_bitcast_fusion.7
  326.0 8.2 convert_reduce_fusion.2
  334.2 3.2 multiply_reduce_fusion.2
  337.4 4.6 fusion.468
  347.2 3.3 fusion.481
  354.9 4.4 copy.172
  394.8 4.6 add_bitcast_fusion.8
  402.8 8.0 multiply_convert_fusion.11
  414.9 4.5 fusion.144
  419.4 3.3 fusion.82
  425.1 5.8 fusion.146
  430.9 19.2 %collective-permute-done.2 = bf16[1024,512]{1,0:T(8,128)(2,1)S(1)} collective-permute-done((bf16[1024,512]{1,0:T(8,128)(2,1)S(1)}, bf16[1024,512]{1,0:T(8,128)(2,1)S(1)}, u32[]{:S(2)}, u32[]{:S(2)}) %collective-permute-start.2) | collective-permute-done | bytes 1048608 | tf_op jit(solution)/shard_map/ppermute | solution.py:12
  451.2 8.6 convert_reduce_fusion.1
  459.8 3.2 multiply_reduce_fusion.1
  465.9 3.3 fusion.482
  508.2 4.6 add_bitcast_fusion.6
  516.2 8.2 multiply_convert_fusion.8
  528.6 3.3 fusion.72
  535.6 4.5 fusion.484
  543.7 4.5 fusion.467
  548.2 10.1 %collective-permute-done.3 = bf16[1024,512]{1,0:T(8,128)(2,1)S(1)} collective-permute-done((bf16[1024,512]{1,0:T(8,128)(2,1)S(1)}, bf16[1024,512]{1,0:T(8,128)(2,1)S(1)}, u32[]{:S(2)}, u32[]{:S(2)}) %collective-permute-start.3) | collective-permute-done | bytes 1048608 | tf_op jit(solution)/shard_map/ppermute | solution.py:12
  559.0 8.0 convert_reduce_fusion
  571.8 3.3 fusion.483
  614.3 4.4 add_bitcast_fusion.4
  622.3 8.5 multiply_convert_fusion.5
  630.9 3.3 fusion.172
  634.2 8.0 add_bitcast_fusion
  642.3 7.5 add_bitcast_fusion.1
  660.0 5.2 add_bitcast_fusion.2
  666.5 8.6 fusion.140
  686.0 4.1 fusion.56
  690.2 62.6 %all-reduce = (f32[1,512]{1,0:T(1,128)}, f32[1,2048]{1,0:T(1,128)}, f32[1,1024]{1,0:T(1,128)}, f32[1,512]{1,0:T(1,128)}, f32[1,512]{1,0:T(1,128)}, /*index=5*/f32[1,2048]{1,0:T(1,128)}, f32[1,512]{1,0:T(1,128)}) all-reduce(f32[1,512]{1,0:T(1,128)S(1)} %bitcast.2969, ...), channel_id=1, replica_groups=mesh['section'=2,'dp'=8,'rep'=2] {'dp','rep'}, use_global_device_ids=true, to_apply=%region_15.16 | all-reduce | flops 7168 | bytes 57344 | tf_op jit(solution)/shard_map/psum | solution.py:293
  758.6 209.1 %all-reduce.4.cloned.1.call-done = (f32[1,512,2048]{2,1,0:T(8,128)}, f32[1,512,1024]{2,1,0:T(8,128)}, f32[1,1024,512]{2,1,0:T(8,128)}, f32[1,512,2048]{2,1,0:T(8,128)}, f32[1,2048,512]{2,1,0:T(8,128)}) async-done(((f32[1,512,2048]{2,1,0:T(8,128)}, f32[1,512,1024]{2,1,0:T(8,128)}, f32[1,1024,512]{2,1,0:T(8,128)}, f32[1,512,2048]{2,1,0:T(8,128)}, f32[1,2048,512]{2,1,0:T(8,128)}), (f32[1,512,2048]{2,1,0:T(8,128)}, ...) | async-done | bytes 16777232 | tf_op jit(solution)/shard_map/psum | solution.py:293
  967.6 4.8 copy.760
  (939 shorter events, 399.6 us)
Async XLA Ops:
  7.2 86.8 %copy-start = (bf16[1,512,2048]{2,1,0:T(8,128)(2,1)S(1)}, bf16[1,512,2048]{2,1,0:T(8,128)(2,1)}, u32[]{:S(2)}) copy-start(bf16[1,512,2048]{2,1,0:T(8,128)(2,1)} %param.26) | copy-start | bytes 6291460
  7.2 960.5 %all-reduce.4.cloned.1.call-start = ((), (), s32[]{:S(2)}) async-start(), calls=%async_computation | async-start | bytes 33554432 | tf_op jit(solution)/shard_map/psum | solution.py:293
  11.5 93.5 %copy-start.137 = (f32[1,1024]{1,0:T(1,128)}, f32[1,1024]{1,0:T(1,128)S(1)}, u32[]{:S(2)}) copy-start(f32[1,1024]{1,0:T(1,128)S(1)} %get-tuple-element.830) | copy-start | bytes 12292
  28.4 30.3 %copy-start.15 = (f32[32,32,1024]{2,0,1:T(8,128)}, f32[32,32,1024]{2,0,1:T(8,128)S(1)}, u32[]{:S(2)}) copy-start(f32[32,32,1024]{2,0,1:T(8,128)S(1)} %copy.195) | copy-start | bytes 12582916
  43.1 13.4 %copy-start.83 = (f32[32,32,1024]{2,1,0:T(8,128)S(1)}, f32[32,32,1024]{2,1,0:T(8,128)}, u32[]{:S(2)}) copy-start(f32[32,32,1024]{2,1,0:T(8,128)} %constant_dynamic-update-slice_fusion.543) | copy-start | bytes 12582916
  44.2 12.2 %copy-start.2 = (f32[32,32,1024]{2,0,1:T(8,128)S(1)}, f32[32,32,1024]{2,0,1:T(8,128)}, u32[]{:S(2)}) copy-start(f32[32,32,1024]{2,0,1:T(8,128)} %copy-done.1) | copy-start | bytes 12582916
  96.5 31.9 %copy-start.166 = (bf16[1,512,2048]{2,1,0:T(8,128)(2,1)S(1)}, bf16[1,512,2048]{2,1,0:T(8,128)(2,1)}, u32[]{:S(2)}) copy-start(bf16[1,512,2048]{2,1,0:T(8,128)(2,1)} %param.19) | copy-start | bytes 6291460
  96.5 31.9 %copy-start.177 = (f32[1,2048]{1,0:T(1,128)S(1)}, f32[1,2048]{1,0:T(1,128)}, u32[]{:S(2)}) copy-start(f32[1,2048]{1,0:T(1,128)} %param.20) | copy-start | bytes 24580
  100.0 28.4 %copy-start.125 = (bf16[1024,512]{1,0:T(8,128)(2,1)}, bf16[1024,512]{1,0:T(8,128)(2,1)S(1)}, u32[]{:S(2)}) copy-start(bf16[1024,512]{1,0:T(8,128)(2,1)S(1)} %add_convert_fusion.5) | copy-start | bytes 3145732
  100.0 27.2 %collective-permute-start = (bf16[1024,512]{1,0:T(8,128)(2,1)S(1)}, bf16[1024,512]{1,0:T(8,128)(2,1)S(1)}, u32[]{:S(2)}, u32[]{:S(2)}) collective-permute-start(bf16[1024,512]{1,0:T(8,128)(2,1)S(1)} %add_convert_fusion.5), channel_id=1, source_target_pairs={{0,16},{1,17},{2,18},{3,19},{4,20},{5,21},{6,22},{7,23},{8,24},{9,... | collective-permute-start | bytes 3145736 | tf_op jit(solution)/shard_map/ppermute | solution.py:12
  105.0 25.8 %copy-start.147 = (f32[1024]{0:T(1024)}, f32[1024]{0:T(1024)S(1)}, u32[]{:S(2)}) copy-start(f32[1024]{0:T(1024)S(1)} %broadcast_select_fusion) | copy-start | bytes 12292
  142.8 30.0 %copy-start.16 = (f32[32,32,1024]{2,0,1:T(8,128)}, f32[32,32,1024]{2,0,1:T(8,128)S(1)}, u32[]{:S(2)}) copy-start(f32[32,32,1024]{2,0,1:T(8,128)S(1)} %copy.193) | copy-start | bytes 12582916
  158.5 12.0 %copy-start.6 = (f32[32,32,1024]{2,0,1:T(8,128)S(1)}, f32[32,32,1024]{2,0,1:T(8,128)}, u32[]{:S(2)}) copy-start(f32[32,32,1024]{2,0,1:T(8,128)} %copy-done.5) | copy-start | bytes 12582916
  216.3 12.1 %copy-start.127 = (bf16[1024,512]{1,0:T(8,128)(2,1)}, bf16[1024,512]{1,0:T(8,128)(2,1)S(1)}, u32[]{:S(2)}) copy-start(bf16[1024,512]{1,0:T(8,128)(2,1)S(1)} %add_convert_fusion.4) | copy-start | bytes 3145732
  216.3 25.9 %collective-permute-start.1 = (bf16[1024,512]{1,0:T(8,128)(2,1)S(1)}, bf16[1024,512]{1,0:T(8,128)(2,1)}, u32[]{:S(2)}, u32[]{:S(2)}) collective-permute-start(bf16[1024,512]{1,0:T(8,128)(2,1)S(1)} %add_convert_fusion.4), channel_id=1, source_target_pairs={{0,16},{1,17},{2,18},{3,19},{4,20},{5,21},{6,22},{7,23},{8,24},{9,... | collective-permute-start | bytes 3145736 | tf_op jit(solution)/shard_map/ppermute | solution.py:12
  258.0 30.0 %copy-start.17 = (f32[32,32,1024]{2,0,1:T(8,128)}, f32[32,32,1024]{2,0,1:T(8,128)S(1)}, u32[]{:S(2)}) copy-start(f32[32,32,1024]{2,0,1:T(8,128)S(1)} %copy.191) | copy-start | bytes 12582916
  273.7 12.0 %copy-start.10 = (f32[32,32,1024]{2,0,1:T(8,128)S(1)}, f32[32,32,1024]{2,0,1:T(8,128)}, u32[]{:S(2)}) copy-start(f32[32,32,1024]{2,0,1:T(8,128)} %copy-done.9) | copy-start | bytes 12582916
  323.0 19.0 %copy-start.18 = (f32[1024,512]{1,0:T(8,128)}, f32[1024,512]{1,0:T(8,128)S(1)}, u32[]{:S(2)}) copy-start(f32[1024,512]{1,0:T(8,128)S(1)} %get-tuple-element.853) | copy-start | bytes 6291460
  326.0 8.2 copy-start.70
  352.9 8.4 copy-start.12
  410.9 8.5 copy-start.54
  410.9 8.5 copy-start.56
  414.9 10.1 %slice-start.4 = ((s8[8388608]{0:T(1024)(128)(4,1)}), s8[4194304]{0:T(1024)(128)(4,1)S(1)}, s32[]{:S(2)}) async-start(s8[8388608]{0:T(1024)(128)(4,1)} %bitcast.2910), calls=%async_computation.5 | async-start | bytes 8388608
  422.8 28.3 %slice-start.6 = ((s8[8388608]{0:T(1024)(128)(4,1)}), s8[4194304]{0:T(1024)(128)(4,1)S(1)}, s32[]{:S(2)}) async-start(s8[8388608]{0:T(1024)(128)(4,1)} %bitcast.2987), calls=%async_computation.7 | async-start | bytes 8388608
  423.5 27.7 %copy-start.164 = (bf16[1,2048,512]{2,1,0:T(8,128)(2,1)S(1)}, bf16[1,2048,512]{2,1,0:T(8,128)(2,1)}, u32[]{:S(2)}) copy-start(bf16[1,2048,512]{2,1,0:T(8,128)(2,1)} %param.28) | copy-start | bytes 6291460
  423.5 27.7 %slice-start.7 = ((s8[8388608]{0:T(1024)(128)(4,1)}), s8[4194304]{0:T(1024)(128)(4,1)S(1)}, s32[]{:S(2)}) async-start(s8[8388608]{0:T(1024)(128)(4,1)} %bitcast.2987), calls=%async_computation.8 | async-start | bytes 8388608
  423.5 26.7 %collective-permute-start.2 = (bf16[1024,512]{1,0:T(8,128)(2,1)S(1)}, bf16[1024,512]{1,0:T(8,128)(2,1)S(1)}, u32[]{:S(2)}, u32[]{:S(2)}) collective-permute-start(bf16[1024,512]{1,0:T(8,128)(2,1)S(1)} %fusion.79), channel_id=1, source_target_pairs={{16,0},{17,1},{18,2},{19,3},{20,4},{21,5},{22,6},{23,7},{24,8},{25... | collective-permute-start | bytes 3145736 | tf_op jit(solution)/shard_map/ppermute | solution.py:12
  451.1 11.8 %copy-start.99 = (bf16[1024,512]{1,0:T(8,128)(2,1)}, bf16[1024,512]{1,0:T(8,128)(2,1)S(1)}, u32[]{:S(2)}) copy-start(bf16[1024,512]{1,0:T(8,128)(2,1)S(1)} %get-tuple-element.39) | copy-start | bytes 3145732
  451.2 8.6 copy-start.44
  451.2 8.6 copy-start.134
  482.5 25.3 %copy-start.129 = (f32[32,1024]{1,0:T(8,128)S(1)}, f32[32,1024]{1,0:T(8,128)}, u32[]{:S(2)}) copy-start(f32[32,1024]{1,0:T(8,128)} %bitcast_multiply_fusion.38) | copy-start | bytes 393220
  516.2 8.2 copy-start.175
  533.8 24.6 %collective-permute-start.3 = (bf16[1024,512]{1,0:T(8,128)(2,1)S(1)}, bf16[1024,512]{1,0:T(8,128)(2,1)S(1)}, u32[]{:S(2)}, u32[]{:S(2)}) collective-permute-start(bf16[1024,512]{1,0:T(8,128)(2,1)S(1)} %get-tuple-element.206), channel_id=1, source_target_pairs={{16,0},{17,1},{18,2},{19,3},{20,4},{21,5},{22,6},{23,7},{24,8},{25... | collective-permute-start | bytes 3145736 | tf_op jit(solution)/shard_map/ppermute | solution.py:12
  540.1 18.8 %slice-start = ((s8[8388608]{0:T(1024)(128)(4,1)}), s8[4194304]{0:T(1024)(128)(4,1)S(1)}, s32[]{:S(2)}) async-start(s8[8388608]{0:T(1024)(128)(4,1)} %bitcast.2906), calls=%async_computation.1 | async-start | bytes 8388608
  543.6 14.7 %copy-start.73 = (bf16[2,1024,512]{2,1,0:T(8,128)(2,1)S(1)}, bf16[2,1024,512]{2,1,0:T(8,128)(2,1)}, u32[]{:S(2)}) copy-start(bf16[2,1024,512]{2,1,0:T(8,128)(2,1)} %param.17) | copy-start | bytes 6291460
  543.7 15.3 %slice-start.1 = ((s8[8388608]{0:T(1024)(128)(4,1)}), s8[4194304]{0:T(1024)(128)(4,1)S(1)}, s32[]{:S(2)}) async-start(s8[8388608]{0:T(1024)(128)(4,1)} %bitcast.2906), calls=%async_computation.2 | async-start | bytes 8388608
  548.2 10.7 %copy-start.165 = (bf16[1,2048,512]{2,1,0:T(8,128)(2,1)S(1)}, bf16[1,2048,512]{2,1,0:T(8,128)(2,1)}, u32[]{:S(2)}) copy-start(bf16[1,2048,512]{2,1,0:T(8,128)(2,1)} %param.28) | copy-start | bytes 6291460
  558.9 10.8 %copy-start.109 = (bf16[1024,512]{1,0:T(8,128)(2,1)}, bf16[1024,512]{1,0:T(8,128)(2,1)S(1)}, u32[]{:S(2)}) copy-start(bf16[1024,512]{1,0:T(8,128)(2,1)S(1)} %get-tuple-element.41) | copy-start | bytes 3145732
  588.4 25.4 %copy-start.128 = (f32[32,1024]{1,0:T(8,128)S(1)}, f32[32,1024]{1,0:T(8,128)}, u32[]{:S(2)}) copy-start(f32[32,1024]{1,0:T(8,128)} %bitcast_multiply_fusion.73) | copy-start | bytes 393220
  618.8 15.3 %slice-start.2 = ((s8[8388608]{0:T(1024)(128)(4,1)}), s8[4194304]{0:T(1024)(128)(4,1)S(1)}, s32[]{:S(2)}) async-start(s8[8388608]{0:T(1024)(128)(4,1)} %bitcast.2908), calls=%async_computation.3 | async-start | bytes 8388608
  622.3 8.6 copy-start.78
  622.3 8.6 copy-start.146
  622.3 11.9 %slice-start.3 = ((s8[8388608]{0:T(1024)(128)(4,1)}), s8[4194304]{0:T(1024)(128)(4,1)S(1)}, s32[]{:S(2)}) async-start(s8[8388608]{0:T(1024)(128)(4,1)} %bitcast.2908), calls=%async_computation.4 | async-start | bytes 8388608
  630.8 11.4 %copy-start.117 = (bf16[1024,1024]{1,0:T(8,128)(2,1)}, bf16[1024,1024]{1,0:T(8,128)(2,1)S(1)}, u32[]{:S(2)}) copy-start(bf16[1024,1024]{1,0:T(8,128)(2,1)S(1)} %get-tuple-element.616) | copy-start | bytes 6291460
  630.8 25.7 %copy-start.65 = (bf16[1024,1024]{1,0:T(8,128)(2,1)}, bf16[1024,1024]{1,0:T(8,128)(2,1)S(1)}, u32[]{:S(2)}) copy-start(bf16[1024,1024]{1,0:T(8,128)(2,1)S(1)} %get-tuple-element.609) | copy-start | bytes 6291460
  630.8 25.7 %copy-start.67 = (bf16[1024,1024]{1,0:T(8,128)(2,1)}, bf16[1024,1024]{1,0:T(8,128)(2,1)S(1)}, u32[]{:S(2)}) copy-start(bf16[1024,1024]{1,0:T(8,128)(2,1)S(1)} %get-tuple-element.610) | copy-start | bytes 6291460
  686.0 66.9 %copy-start.113 = (bf16[1024,512]{1,0:T(8,128)(2,1)S(1)}, bf16[1024,512]{1,0:T(8,128)(2,1)}, u32[]{:S(2)}) copy-start(bf16[1024,512]{1,0:T(8,128)(2,1)} %copy-done.112) | copy-start | bytes 3145732
  686.0 66.9 %copy-start.144 = (f32[1024]{0:T(1024)S(1)}, f32[1024]{0:T(1024)}, u32[]{:S(2)}) copy-start(f32[1024]{0:T(1024)} %get-tuple-element.831) | copy-start | bytes 12292
  (156 other events, 576.4 us)
Sparse Core Ops, SparseCore 0:
  665.3 302.2 all-reduce.3
where the time goes:
time: 996 us; the launch traced here: 989 us
  other arithmetic  299 us (30%)
  waiting for transfers between devices  267 us (27%)
  matrix products  180 us (18%)
  local copies, waits for them, and re-layouts  149 us (15%)
  blocking collectives  62.6 us (6%)
  between operations  18.6 us (2%)
  starting transfers between devices  13.4 us (1%)
    psum x1, waiting for transfers between devices, body(): lax.psum((sum_g_one, sum_w_gate, sum_b_gate, sum_w_cand, sum_b_cand, sum_...  209 us
    unnamed x232, other arithmetic  191 us
    unnamed x594, local copies, waits for them, and re-layouts  91.8 us
    dot_general x15, matrix products, weight_grad(): lax.dot_general(operand, gradient, (((0,), (0,)), ((), ())), preferred_el...  63.9 us
    psum x1, blocking collectives, body(): lax.psum((sum_g_one, sum_w_gate, sum_b_gate, sum_w_cand, sum_b_cand, sum_...  62.6 us
    dot_general x15, matrix products, matmul_back(): lax.dot_general(operand, weight, (((1,), (1,)), ((), ())), preferred_elem...  58.2 us
    dot_general x15, matrix products, matmul(): return jnp.dot(operand, weight, preferred_element_type=jnp.float32)  58 us
    ppermute x4, waiting for transfers between devices, shifted(): return lax.ppermute(x, axis, pairs)  57.8 us
  transfers between devices with their start and end apart: 5, of which 5 were waited for; matrix products, arithmetic and copies ran while one was open for 6% of the time, Pallas kernels for 0%

commit v1 on v0

v1 whole, which is shorter than its diff:
```python
import functools
import math

import jax
import jax.numpy as jnp
from jax import lax
from jax.experimental import pallas as pl
from jax.experimental.pallas import tpu as pltpu
from jax.sharding import PartitionSpec as P

EPS = 1e-06
F32 = jnp.float32
BF16 = jnp.bfloat16
CHUNK = 128
LANES = 8
WIDTH = 256
GELU_A = math.sqrt(2.0 / math.pi)
GELU_B = 0.044715
LN4 = math.log(4.0)
EXP_TOP = 85.6
VMEM_LIMIT = 60 * 1024 * 1024


def dot(a, b):
    return jnp.dot(a, b, preferred_element_type=F32)


def dot_nt(a, b):
    return lax.dot_general(a, b, (((1,), (1,)), ((), ())), preferred_element_type=F32)


def inv_scale(values):
    return lax.rsqrt(jnp.mean(values * values, axis=-1, keepdims=True) + EPS)


def partner_barrier_signal(partner):
    pl.semaphore_signal(
        pltpu.get_barrier_semaphore(),
        inc=1,
        device_id={"section": partner},
        device_id_type=pl.DeviceIdType.MESH,
    )


def chunk_copy(send, recv, send_sem, recv_sem, slot, partner):
    return pltpu.make_async_remote_copy(
        src_ref=send.at[slot],
        dst_ref=recv.at[slot],
        send_sem=send_sem.at[slot],
        recv_sem=recv_sem.at[slot],
        device_id={"section": partner},
        device_id_type=pl.DeviceIdType.MESH,
    )


def segment_index(width, per_row):
    return lax.broadcasted_iota(jnp.int32, (LANES, width), 0) % per_row


def forward_kernel(
    steps,
    per_row,
    tok,
    keep,
    perm,
    perm_t,
    g_one,
    w_gate,
    b_gate,
    w_cand,
    b_cand,
    w_out,
    b_out,
    g_two,
    w_up,
    b_up,
    w_down,
    b_down,
    out,
    x_o,
    normed_o,
    decay_o,
    slope_forget_o,
    slope_inward_o,
    slope_cand_o,
    state_o,
    middle_o,
    normed_two_o,
    active_o,
    slope_up_o,
    send,
    recv,
    carry,
    send_sem,
    recv_sem,
):
    c = pl.program_id(0)
    section = lax.axis_index("section")
    partner = 1 - section
    rows, chunk, width = tok.shape
    tokens = rows * chunk
    hidden = w_cand.shape[1]
    ff = w_up.shape[1]
    span = tokens // LANES

    @pl.when(c == 0)
    def _():
        partner_barrier_signal(partner)
        carry[...] = jnp.zeros_like(carry)
        pl.semaphore_wait(pltpu.get_barrier_semaphore(), 1)

    @pl.when(section == 0)
    def _():
        x_o[0] = dot(perm[...], tok[...].reshape(tokens, width)).astype(BF16)

    @pl.when(section == 1)
    def _():
        chunk_copy(send, recv, send_sem, recv_sem, c, partner).wait_recv()
        x_o[0] = recv[c]

    x = x_o[0].astype(F32)
    normed = (x * inv_scale(x) * g_one[...]).astype(BF16)
    normed_o[0] = normed
    mixed = jnp.zeros((tokens, width), F32)
    which = segment_index(WIDTH, per_row)
    for at in range(0, hidden, WIDTH):
        cols = slice(at, at + WIDTH)
        cols_in = slice(hidden + at, hidden + at + WIDTH)
        pre_f = dot(normed, w_gate[:, cols])
        pre_i = dot(normed, w_gate[:, cols_in])
        cand = dot(normed, w_cand[:, cols]) + b_cand[:, cols]
        u = jnp.exp(jnp.minimum((-LN4 - b_gate[:, cols]) - pre_f, EXP_TOP))
        v = jnp.exp(jnp.minimum((-LN4 - b_gate[:, cols_in]) - pre_i, EXP_TOP))
        d = 1.0 / (0.5 + u + v)
        ratio_f = (0.25 + v) * d
        ratio_i = (0.25 + u) * d
        keep_w = jnp.concatenate([keep[0]] * (WIDTH // 128), axis=1)
        decay = ratio_f * keep_w
        drive = ratio_i * cand
        decay_o[0, :, cols] = decay
        slope_cand_o[0, :, cols] = ratio_i.astype(BF16)
        product = decay[0:LANES]
        accum = drive[0:LANES]
        for j in range(1, span):
            r = slice(j * LANES, (j + 1) * LANES)
            accum = decay[r] * accum + drive[r]
            product = decay[r] * product
        incoming = carry[:, cols]
        for q in range(1, per_row):
            nxt = pltpu.roll(product * incoming + accum, 1, 0)
            incoming = jnp.where(which == q, nxt, incoming)
        carry[:, cols] = pltpu.roll(product * incoming + accum, LANES - per_row + 1, 0)
        state = incoming
        before = []
        after = []
        for j in range(span):
            r = slice(j * LANES, (j + 1) * LANES)
            before.append(state)
            state = decay[r] * state + drive[r]
            after.append(state)
        state_low = jnp.concatenate(after, axis=0).astype(BF16)
        state_o[0, :, cols] = state_low
        lever = keep_w * jnp.concatenate(before, axis=0) - cand
        slope_forget_o[0, :, cols] = (lever * (u * d) * ratio_f).astype(BF16)
        slope_inward_o[0, :, cols] = (-lever * (v * d) * ratio_i).astype(BF16)
        mixed = mixed + dot(state_low, w_out[cols, :])
    middle = x + (mixed + b_out[...])
    middle_o[0] = middle
    normed_two = (middle * inv_scale(middle) * g_two[...]).astype(BF16)
    normed_two_o[0] = normed_two
    down = jnp.zeros((tokens, width), F32)
    for at in range(0, ff, WIDTH):
        cols = slice(at, at + WIDTH)
        up = dot(normed_two, w_up[:, cols]) + b_up[:, cols]
        square = up * up
        half = 0.5 + 0.5 * jnp.tanh(up * (GELU_A + (GELU_A * GELU_B) * square))
        act = up * half
        active = act.astype(BF16)
        active_o[0, :, cols] = active
        slope = half + act * (1.0 - half) * (2 * GELU_A + (6 * GELU_A * GELU_B) * square)
        slope_up_o[0, :, cols] = slope.astype(BF16)
        down = down + dot(active, w_down[cols, :])
    low = (middle + (down + b_down[...])).astype(BF16)

    @pl.when(section == 0)
    def _():
        send[c] = low
        chunk_copy(send, recv, send_sem, recv_sem, c, partner).start()

    out[...] = dot(perm_t[...], low).astype(BF16).reshape(out.shape)

    @pl.when((c == steps - 1) & (section == 0))
    def _():
        for slot in range(steps):
            chunk_copy(send, recv, send_sem, recv_sem, slot, partner).wait_send()


def backward_kernel(
    steps,
    per_row,
    cot,
    x_i,
    decay_i,
    slope_forget_i,
    slope_inward_i,
    slope_cand_i,
    middle_i,
    slope_up_i,
    perm,
    perm_t,
    g_one,
    w_gate,
    w_cand,
    w_out,
    g_two,
    w_up,
    w_down,
    grad_in,
    down_o,
    up_o,
    mix_o,
    gate_o,
    cand_o,
    small_o,
    send,
    recv,
    carry,
    send_sem,
    recv_sem,
):
    c = pl.program_id(0)
    section = lax.axis_index("section")
    partner = 1 - section
    rows, chunk, width = cot.shape
    tokens = rows * chunk
    hidden = w_cand.shape[1]
    ff = w_up.shape[1]
    span = tokens // LANES
    at_b_gate = width
    at_b_cand = at_b_gate + 2 * hidden
    at_b_out = at_b_cand + hidden
    at_g_two = at_b_out + width
    at_b_up = at_g_two + width
    at_b_down = at_b_up + ff

    def add_small(at, values):
        n = values.shape[1]
        part = jnp.sum(values.reshape(-1, LANES, n), axis=0)
        small_o[:, at : at + n] += part

    @pl.when(c == 0)
    def _():
        partner_barrier_signal(partner)
        carry[...] = jnp.zeros_like(carry)
        small_o[...] = jnp.zeros_like(small_o)
        pl.semaphore_wait(pltpu.get_barrier_semaphore(), 1)

    @pl.when(section == 1)
    def _():
        down_o[0] = dot(perm[...], cot[...].reshape(tokens, width)).astype(BF16)

    @pl.when(section == 0)
    def _():
        chunk_copy(send, recv, send_sem, recv_sem, c, partner).wait_recv()
        down_o[0] = recv[c]

    grad_down = down_o[0]
    dy = grad_down.astype(F32)
    add_small(at_b_down, dy)
    q = jnp.zeros((tokens, width), F32)
    for at in range(0, ff, WIDTH):
        cols = slice(at, at + WIDTH)
        grad_up = dot_nt(grad_down, w_down[cols, :]) * slope_up_i[0, :, cols].astype(F32)
        add_small(at_b_up + at, grad_up)
        grad_up = grad_up.astype(BF16)
        up_o[0, :, cols] = grad_up
        q = q + dot_nt(grad_up, w_up[:, cols])
    middle = middle_i[0]
    r = inv_scale(middle)
    scaled = middle * r
    add_small(at_g_two, q * scaled)
    weighted = q * g_two[...]
    grad_middle = dy + r * (
        weighted - scaled * jnp.mean(weighted * scaled, axis=-1, keepdims=True)
    )
    add_small(at_b_out, grad_middle)
    grad_mix = grad_middle.astype(BF16)
    mix_o[0] = grad_mix
    p = jnp.zeros((tokens, width), F32)
    which = segment_index(WIDTH, per_row)
    for at in range(0, hidden, WIDTH):
        cols = slice(at, at + WIDTH)
        cols_in = slice(hidden + at, hidden + at + WIDTH)
        grad_state = dot_nt(grad_mix, w_out[cols, :])
        decay = decay_i[0, :, cols]
        last = slice((span - 1) * LANES, span * LANES)
        product = decay[last]
        accum = decay[last] * grad_state[last]
        for j in range(span - 2, -1, -1):
            rj = slice(j * LANES, (j + 1) * LANES)
            accum = decay[rj] * (grad_state[rj] + accum)
            product = decay[rj] * product
        incoming = carry[:, cols]
        for k in range(per_row - 2, -1, -1):
            nxt = pltpu.roll(product * incoming + accum, LANES - 1, 0)
            incoming = jnp.where(which == k, nxt, incoming)
        carry[:, cols] = pltpu.roll(product * incoming + accum, per_row - 1, 0)
        later = incoming
        parts = [None] * span
        for j in range(span - 1, -1, -1):
            rj = slice(j * LANES, (j + 1) * LANES)
            carried = grad_state[rj] + later
            parts[j] = carried
            later = decay[rj] * carried
        carried = jnp.concatenate(parts, axis=0)
        grad_forget = carried * slope_forget_i[0, :, cols].astype(F32)
        grad_inward = carried * slope_inward_i[0, :, cols].astype(F32)
        grad_cand = carried * slope_cand_i[0, :, cols].astype(F32)
        add_small(at_b_gate + at, grad_forget)
        add_small(at_b_gate + hidden + at, grad_inward)
        add_small(at_b_cand + at, grad_cand)
        grad_forget = grad_forget.astype(BF16)
        grad_inward = grad_inward.astype(BF16)
        grad_cand = grad_cand.astype(BF16)
        gate_o[0, :, cols] = grad_forget
        gate_o[0, :, cols_in] = grad_inward
        cand_o[0, :, cols] = grad_cand
        p = p + dot_nt(grad_forget, w_gate[:, cols])
        p = p + dot_nt(grad_inward, w_gate[:, cols_in])
        p = p + dot_nt(grad_cand, w_cand[:, cols])
    x = x_i[0].astype(F32)
    r = inv_scale(x)
    scaled = x * r
    add_small(0, p * scaled)
    weighted = p * g_one[...]
    grad_input = grad_middle + r * (
        weighted - scaled * jnp.mean(weighted * scaled, axis=-1, keepdims=True)
    )
    low = grad_input.astype(BF16)

    @pl.when(section == 1)
    def _():
        send[c] = low
        chunk_copy(send, recv, send_sem, recv_sem, c, partner).start()

    rest = jnp.where(section == 0, grad_input - low.astype(F32), 0.0).astype(BF16)
    grad_in[...] = (dot(perm_t[...], low) + dot(perm_t[...], rest)).reshape(grad_in.shape)

    @pl.when((c == steps - 1) & (section == 1))
    def _():
        for slot in range(steps):
            chunk_copy(send, recv, send_sem, recv_sem, slot, partner).wait_send()


def whole(array):
    zeros = (0,) * array.ndim
    return pl.BlockSpec(array.shape, lambda c: zeros, pipeline_mode=pl.Buffered(1))


def run_forward(tokens, keep, perm, perm_t, weights, chunk):
    rows, seq, width = tokens.shape
    steps = seq // chunk
    size = rows * chunk
    hidden = weights[3].shape[1]
    ff = weights[8].shape[1]

    def saved(columns, dtype):
        shape = jax.ShapeDtypeStruct((steps, size, columns), dtype)
        return shape, pl.BlockSpec((1, size, columns), lambda c: (c, 0, 0))

    out = (
        jax.ShapeDtypeStruct((1, rows, seq, width), BF16),
        pl.BlockSpec((1, rows, chunk, width), lambda c: (0, 0, c, 0)),
    )
    outs = [
        out,
        saved(width, BF16),
        saved(width, BF16),
        saved(hidden, F32),
        saved(hidden, BF16),
        saved(hidden, BF16),
        saved(hidden, BF16),
        saved(hidden, BF16),
        saved(width, F32),
        saved(width, BF16),
        saved(ff, BF16),
        saved(ff, BF16),
    ]
    return pl.pallas_call(
        functools.partial(forward_kernel, steps, LANES // rows),
        grid=(steps,),
        out_shape=[o[0] for o in outs],
        in_specs=[
            pl.BlockSpec((rows, chunk, width), lambda c: (0, c, 0)),
            pl.BlockSpec((1, size, 128), lambda c: (c, 0, 0)),
            whole(perm),
            whole(perm_t),
        ]
        + [whole(w) for w in weights],
        out_specs=[o[1] for o in outs],
        scratch_shapes=[
            pltpu.VMEM((steps, size, width), BF16),
            pltpu.VMEM((steps, size, width), BF16),
            pltpu.VMEM((LANES, hidden), F32),
            pltpu.SemaphoreType.DMA((steps,)),
            pltpu.SemaphoreType.DMA((steps,)),
        ],
        compiler_params=pltpu.CompilerParams(
            collective_id=0, has_side_effects=True, vmem_limit_bytes=VMEM_LIMIT
        ),
        name="forward_block",
    )(tokens, keep, perm, perm_t, *weights)


def run_backward(cotangent, saved_vals, perm, perm_t, weights, chunk):
    rows, seq, width = cotangent.shape
    steps = seq // chunk
    size = rows * chunk
    g_one, w_gate, _, w_cand, _, w_out, _, g_two, w_up, _, w_down, _ = weights
    hidden = w_cand.shape[1]
    ff = w_up.shape[1]
    small = 4 * width + 3 * hidden + ff

    def back(c):
        return (steps - 1 - c, 0, 0)

    def given(columns, dtype):
        shape = jax.ShapeDtypeStruct((steps, size, columns), dtype)
        return shape, pl.BlockSpec((1, size, columns), back)

    outs = [
        (
            jax.ShapeDtypeStruct((1, rows, seq, width), F32),
            pl.BlockSpec((1, rows, chunk, width), lambda c: (0, 0, steps - 1 - c, 0)),
        ),
        given(width, BF16),
        given(ff, BF16),
        given(width, BF16),
        given(2 * hidden, BF16),
        given(hidden, BF16),
        (
            jax.ShapeDtypeStruct((LANES, small), F32),
            pl.BlockSpec((LANES, small), lambda c: (0, 0)),
        ),
    ]
    consts = (perm, perm_t, g_one, w_gate, w_cand, w_out, g_two, w_up, w_down)
    return pl.pallas_call(
        functools.partial(backward_kernel, steps, LANES // rows),
        grid=(steps,),
        out_shape=[o[0] for o in outs],
        in_specs=[pl.BlockSpec((rows, chunk, width), lambda c: (0, steps - 1 - c, 0))]
        + [pl.BlockSpec((1, size, v.shape[2]), back) for v in saved_vals]
        + [whole(w) for w in consts],
        out_specs=[o[1] for o in outs],
        scratch_shapes=[
            pltpu.VMEM((steps, size, width), BF16),
            pltpu.VMEM((steps, size, width), BF16),
            pltpu.VMEM((LANES, hidden), F32),
            pltpu.SemaphoreType.DMA((steps,)),
            pltpu.SemaphoreType.DMA((steps,)),
        ],
        compiler_params=pltpu.CompilerParams(
            collective_id=1, has_side_effects=True, vmem_limit_bytes=VMEM_LIMIT
        ),
        name="backward_block",
    )(cotangent, *saved_vals, *consts)


def weight_grad(operand, gradient):
    a = operand.reshape(-1, operand.shape[-1])
    b = gradient.reshape(-1, gradient.shape[-1])
    return lax.dot_general(a, b, (((0,), (0,)), ((), ())), preferred_element_type=F32)


def local_grads(tokens, resets, cotangent, stacked):
    weights = tuple(w if w.ndim == 2 else w[0] for w in stacked)
    rows, seq, width = tokens.shape
    chunk = min(CHUNK, seq)
    steps = seq // chunk
    size = rows * chunk
    per_row = LANES // rows
    span = size // LANES
    keep = (1 - resets).astype(F32).reshape(rows, steps, per_row, span)
    keep = keep.transpose(1, 3, 0, 2).reshape(steps, size, 1)
    keep = jnp.broadcast_to(keep, (steps, size, 128))
    at = lax.broadcasted_iota(jnp.int32, (size, size), 0)
    source = lax.broadcasted_iota(jnp.int32, (size, size), 1)
    perm = (source == (at % LANES) * span + at // LANES).astype(BF16)
    perm_t = (at == (source % LANES) * span + source // LANES).astype(BF16)
    (
        block_out,
        x,
        normed,
        decay,
        slope_forget,
        slope_inward,
        slope_cand,
        state_low,
        middle,
        normed_two,
        active,
        slope_up,
    ) = run_forward(tokens, keep, perm, perm_t, weights, chunk)
    grad_in, g_down, g_up, g_mix, g_gate, g_cand, small = run_backward(
        cotangent,
        (x, decay, slope_forget, slope_inward, slope_cand, middle, slope_up),
        perm,
        perm_t,
        weights,
        chunk,
    )
    large = (
        weight_grad(normed, g_gate),
        weight_grad(normed, g_cand),
        weight_grad(state_low, g_mix),
        weight_grad(normed_two, g_up),
        weight_grad(active, g_down),
    )
    return block_out, grad_in, large, jnp.sum(small, axis=0)


def split_small(small, width, hidden, ff):
    sizes = (width, 2 * hidden, hidden, width, width, ff, width)
    out = []
    at = 0
    for n in sizes:
        out.append(small[at : at + n])
        at += n
    return out


def body(tokens, resets, cotangent, *stacked):
    block_out, grad_in, large, small = local_grads(tokens, resets, cotangent, stacked)
    width = tokens.shape[2]
    hidden = stacked[3].shape[2]
    ff = stacked[8].shape[2]
    sums = lax.psum(tuple(g.astype(BF16) for g in large) + (small,), ("dp", "rep"))
    w_gate, w_cand, w_out, w_up, w_down = (s.astype(F32) for s in sums[:5])
    g_one, b_gate, b_cand, b_out, g_two, b_up, b_down = split_small(sums[5], width, hidden, ff)
    grads = (g_one, w_gate, b_gate, w_cand, b_cand, w_out, b_out, g_two, w_up, b_up, w_down, b_down)
    return (block_out, grad_in) + tuple(g[None] for g in grads)


def solution(mesh):
    vector = P("section", None)
    matrix = P("section", None, None)
    weight_specs = (
        vector,
        matrix,
        vector,
        matrix,
        vector,
        matrix,
        vector,
        vector,
        matrix,
        vector,
        matrix,
        vector,
    )
    tokens = P(("dp", "rep"), None, None)
    by_rows = P("section", ("dp", "rep"), None, None)
    return jax.shard_map(
        body,
        mesh=mesh,
        in_specs=(tokens, P(("dp", "rep"), None), tokens) + weight_specs,
        out_specs=(by_rows, by_rows) + weight_specs,
        check_vma=False,
    )
```

time: 996 us -> 374 us (0.38)
  other arithmetic: 299 us -> 14.3 us
  waiting for transfers between devices: 267 us -> 106 us
  matrix products: 180 us -> 29.9 us
  local copies, waits for them, and re-layouts: 149 us -> 10 us
  Pallas kernels: 0 us -> 136 us
  starting transfers between devices: 13.4 us -> 0.04 us
    unnamed x232 -> x2, other arithmetic: 191 us -> 0.01 us
    dot_general x45 -> x5, matrix products: 180 us -> 29.9 us  [weight_grad(): lax.dot_general(a, b, (((0,), (0,)), ((), ())), preferred_element_type=F32)]
    pallas_call x0 -> x2, Pallas kernels: none -> 136 us  [the longest x1 71.8 us: run_backward(): pl.pallas_call(functools.partial(backward_kernel, steps, LANES // rows),...]
    psum x1, waiting for transfers between devices: 209 us -> 106 us  [body(): lax.psum(tuple((g.astype(BF16) for g in large)) + (small,), ('dp', 'rep'))]
    unnamed x594 -> x34, local copies, waits for them, and re-layouts: 91.8 us -> 6.66 us
    ppermute x4 -> x0, waiting for transfers between devices: 57.8 us -> none  [shifted(): return lax.ppermute(x, axis, pairs)]
    transpose x6 -> x0, other arithmetic: 44.4 us -> none  [block_scan(): exclusive = exclusive.transpose((1, 0, 2)).reshape((seq_len, width))]
    another operation x12 -> x0, other arithmetic: 32.9 us -> none
  transfers between devices with their start and end apart: 5 -> 1, of which waited for: 5 -> 1; matrix products, arithmetic and copies ran while one was open for 6% -> 0% of each run, Pallas kernels for 0% -> 0%
where the time goes in v1:
time: 374 us
  Pallas kernels  136 us (36%)
  waiting for transfers between devices  106 us (28%)
  blocking collectives  63.4 us (17%)
  matrix products  29.9 us (8%)
  other arithmetic  14.3 us (4%)
  between operations  14.2 us (4%)
  local copies, waits for them, and re-layouts  10 us (3%)
    psum x1, waiting for transfers between devices, body(): lax.psum(tuple((g.astype(BF16) for g in large)) + (small,), ('dp', 'rep'))  106 us
    pallas_call x1, Pallas kernels, run_backward(): pl.pallas_call(functools.partial(backward_kernel, steps, LANES // rows),...  71.8 us
    pallas_call x1, Pallas kernels, run_forward(): pl.pallas_call(functools.partial(forward_kernel, steps, LANES // rows), g...  63.8 us
    psum x1, blocking collectives, body(): lax.psum(tuple((g.astype(BF16) for g in large)) + (small,), ('dp', 'rep'))  63.4 us
    dot_general x5, matrix products, weight_grad(): lax.dot_general(a, b, (((0,), (0,)), ((), ())), preferred_element_type=F32)  29.9 us
    broadcast_in_dim x5, other arithmetic, body(): return (block_out, grad_in) + tuple((g[None] for g in grads))  12.5 us
  transfers between devices with their start and end apart: 1, of which 1 were waited for; matrix products, arithmetic and copies ran while one was open for 0% of the time, Pallas kernels for 0%

profile of v1, /device:TPU:0, one launch (start us, length us, event | category | flops | bytes accessed | tf_op | source)
XLA Modules:
  0.0 373.8 jit_solution(8546588709185664859)
XLA Ops:
  7.2 0.0 all-reduce.3.cloned.1.call-start
  7.3 0.7 subtract_convert_fusion
  8.0 0.1 reshape.11
  8.1 0.1 copy.35
  8.2 0.1 copy.36
  8.2 0.9 fusion.6
  9.2 1.3 broadcast_in_dim.59.keep
  10.5 63.8 %forward_block.1 = (bf16[1,2,1024,512]{3,2,1,0:T(8,128)(2,1)}, bf16[8,256,512]{2,1,0:T(8,128)(2,1)}, bf16[8,256,512]{2,1,0:T(8,128)(2,1)}, f32[8,256,1024]{2,1,0...) custom-call(bf16[2,1024,512]{2,1,0:T(8,128)(2,1)} %tok.1, ...), custom_call_target="tpu_custom_call" | custom-call | tf_op jit(solution)/shard_map/forward_block/pallas_call | solution.py:389
  74.4 0.0 copy-start.9
  74.4 71.8 %backward_block.1 = (f32[1,2,1024,512]{3,2,1,0:T(8,128)}, bf16[8,256,512]{2,1,0:T(8,128)(2,1)}, bf16[8,256,2048]{2,1,0:T(8,128)(2,1)}, bf16[8,256,512]{2,1,0:T(8...) custom-call(bf16[2,1024,512]{2,1,0:T(8,128)(2,1)} %cot.1, ...), custom_call_target="tpu_custom_call" | custom-call | tf_op jit(solution)/shard_map/backward_block/pallas_call | solution.py:447
  146.1 0.0 copy-done.9
  146.2 0.0 slice-start
  146.2 5.7 %fusion.3 = bf16[1,512,1024]{2,1,0:T(8,128)(2,1)} fusion(bf16[8,256,512]{2,1,0:T(8,128)(2,1)S(1)} %copy-done.9, bf16[8,256,1024]{2,1,0:T(8,128)(2,1)} %get-tuple-element.45), kind=kOutput, calls=%fused_computation.8 | convolution fusion | flops 2148007936 | bytes 7340032 | tf_op jit(solution)/shard_map/dot_general | solution.py:472
  151.8 9.4 %fusion = bf16[1,512,2048]{2,1,0:T(8,128)(2,1)} fusion(bf16[8,256,512]{2,1,0:T(8,128)(2,1)S(1)} %copy-done.9, bf16[8,256,2048]{2,1,0:T(8,128)(2,1)} %get-tuple-element.44), kind=kOutput, calls=%fused_computation.3 | convolution fusion | flops 4296015872 | bytes 12582912 | tf_op jit(solution)/shard_map/dot_general | solution.py:472
  161.3 0.0 slice-done
  161.3 0.0 slice-done.1
  161.3 0.0 copy-done.11
  161.3 0.0 slice-start.3
  161.3 0.0 copy-start.8
  161.3 5.7 %fusion.2 = bf16[1,2048,512]{2,1,0:T(8,128)(2,1)} fusion(bf16[8,256,2048]{2,1,0:T(8,128)(2,1)S(1)} %bitcast.74, bf16[8,256,512]{2,1,0:T(8,128)(2,1)S(1)} %copy-done.11), kind=kOutput, calls=%fused_computation.5 | convolution fusion | flops 4296015872 | bytes 12582912 | tf_op jit(solution)/shard_map/dot_general | solution.py:472
  167.0 0.0 slice-done.2
  167.0 0.0 slice-done.3
  167.0 0.0 copy-done.8
  167.1 0.0 copy-start.7
  167.1 0.0 copy-start.10
  167.1 5.7 %fusion.1 = bf16[1,512,2048]{2,1,0:T(8,128)(2,1)} fusion(bf16[8,256,512]{2,1,0:T(8,128)(2,1)S(1)} %copy-done.8, bf16[8,256,2048]{2,1,0:T(8,128)(2,1)S(1)} %bitcast.76), kind=kOutput, calls=%fused_computation.4 | convolution fusion | flops 4296015872 | bytes 12582912 | tf_op jit(solution)/shard_map/dot_general | solution.py:472
  172.8 0.0 copy-done.7
  172.8 0.0 copy-done.10
  172.8 3.3 fusion.4
  176.1 0.0 all-reduce.3.cloned.1.call-update
  176.2 0.9 copy-done.6
  177.1 0.1 reduce_sum.9
  177.1 63.4 %psum.42 = f32[7168]{0:T(1024)S(1)} all-reduce(f32[7168]{0:T(1024)S(1)} %reduce_sum.9), channel_id=1, replica_groups=mesh['section'=2,'dp'=8,'rep'=2] {'dp','rep'}, use_global_device_ids=true, to_apply=%region_1.2 | all-reduce | flops 7168 | bytes 57344 | tf_op jit(solution)/shard_map/psum | solution.py:537
  240.5 0.6 slice.30
  241.1 0.6 fusion.9
  241.7 0.6 fusion.10
  242.3 106.4 %all-reduce.3.cloned.1.call-done = (bf16[1,512,2048]{2,1,0:T(8,128)(2,1)}, bf16[1,512,1024]{2,1,0:T(8,128)(2,1)}, bf16[1,1024,512]{2,1,0:T(8,128)(2,1)}, bf16[1,...) async-done(((bf16[1,512,2048]{2,1,0:T(8,128)(2,1)}, bf16[1,512,1024]{2,1,0:T(8,128)(2,1)}, bf16[1,1024,512]{2,1,0:T(8,128)(2,1)}, bf16[1,512,2048]{2,1,0:T(8,128)(2,1)}, ...) | async-done | bytes 8388624 | tf_op jit(solution)/shard_map/psum | solution.py:537
  348.7 4.2 %broadcast_in_dim.62 = f32[1,512,2048]{2,1,0:T(8,128)} convert(bf16[1,512,2048]{2,1,0:T(8,128)(2,1)} %get-tuple-element.52) | non-fusion elementwise | flops 1048576 | bytes 6291456 | tf_op jit(solution)/shard_map/broadcast_in_dim | solution.py:541
  352.9 0.0 copy-done.5
  352.9 1.6 broadcast_in_dim.65
  354.5 1.6 broadcast_in_dim.68
  356.1 0.7 copy-done.2
  356.8 2.5 broadcast_in_dim.72
  359.4 2.6 broadcast_in_dim.75
  362.0 0.0 copy-done.3
  362.0 1.3 copy.54
  363.3 1.6 copy-done
  364.9 2.0 copy.55
  (17 shorter events, 0.0 us)
Async XLA Ops:
  7.2 341.5 %all-reduce.3.cloned.1.call-start = ((), (), s32[]{:S(2)}) async-start(), calls=%async_computation | async-start | bytes 16777216 | tf_op jit(solution)/shard_map/psum | solution.py:537
  74.4 71.8 %copy-start.9 = (bf16[8,256,512]{2,1,0:T(8,128)(2,1)S(1)}, bf16[8,256,512]{2,1,0:T(8,128)(2,1)}, u32[]{:S(2)}) copy-start(bf16[8,256,512]{2,1,0:T(8,128)(2,1)} %get-tuple-element.43) | copy-start | bytes 6291460
  146.2 15.1 %slice-start = ((s8[8388608]{0:T(1024)(128)(4,1)}), s8[4194304]{0:T(1024)(128)(4,1)S(1)}, s32[]{:S(2)}) async-start(s8[8388608]{0:T(1024)(128)(4,1)} %bitcast.73), calls=%async_computation.1 | async-start | bytes 8388608
  151.8 9.5 %slice-start.1 = ((s8[8388608]{0:T(1024)(128)(4,1)}), s8[4194304]{0:T(1024)(128)(4,1)S(1)}, s32[]{:S(2)}) async-start(s8[8388608]{0:T(1024)(128)(4,1)} %bitcast.73), calls=%async_computation.2 | async-start | bytes 8388608
  151.8 9.5 %copy-start.11 = (bf16[8,256,512]{2,1,0:T(8,128)(2,1)S(1)}, bf16[8,256,512]{2,1,0:T(8,128)(2,1)}, u32[]{:S(2)}) copy-start(bf16[8,256,512]{2,1,0:T(8,128)(2,1)} %get-tuple-element.51) | copy-start | bytes 6291460
  151.8 15.2 %slice-start.2 = ((s8[8388608]{0:T(1024)(128)(4,1)}), s8[4194304]{0:T(1024)(128)(4,1)S(1)}, s32[]{:S(2)}) async-start(s8[8388608]{0:T(1024)(128)(4,1)} %bitcast.75), calls=%async_computation.3 | async-start | bytes 8388608
  161.3 5.7 %slice-start.3 = ((s8[8388608]{0:T(1024)(128)(4,1)}), s8[4194304]{0:T(1024)(128)(4,1)S(1)}, s32[]{:S(2)}) async-start(s8[8388608]{0:T(1024)(128)(4,1)} %bitcast.75), calls=%async_computation.4 | async-start | bytes 8388608
  161.3 5.7 %copy-start.8 = (bf16[8,256,512]{2,1,0:T(8,128)(2,1)S(1)}, bf16[8,256,512]{2,1,0:T(8,128)(2,1)}, u32[]{:S(2)}) copy-start(bf16[8,256,512]{2,1,0:T(8,128)(2,1)} %get-tuple-element.48) | copy-start | bytes 6291460
  167.1 5.7 %copy-start.7 = (bf16[8,256,1024]{2,1,0:T(8,128)(2,1)S(1)}, bf16[8,256,1024]{2,1,0:T(8,128)(2,1)}, u32[]{:S(2)}) copy-start(bf16[8,256,1024]{2,1,0:T(8,128)(2,1)} %get-tuple-element.46) | copy-start | bytes 12582916
  167.1 5.7 %copy-start.10 = (bf16[8,256,512]{2,1,0:T(8,128)(2,1)S(1)}, bf16[8,256,512]{2,1,0:T(8,128)(2,1)}, u32[]{:S(2)}) copy-start(bf16[8,256,512]{2,1,0:T(8,128)(2,1)} %get-tuple-element.47) | copy-start | bytes 6291460
  176.1 0.9 copy-start.6
  348.7 4.2 %copy-start.5 = (bf16[1,512,1024]{2,1,0:T(8,128)(2,1)S(1)}, bf16[1,512,1024]{2,1,0:T(8,128)(2,1)}, u32[]{:S(2)}) copy-start(bf16[1,512,1024]{2,1,0:T(8,128)(2,1)} %get-tuple-element.53) | copy-start | bytes 3145732
  352.9 1.6 copy-start.4
  354.5 2.3 copy-start.2
  356.8 2.5 copy-start.1
  359.4 2.6 copy-start.3
  362.0 2.9 copy-start
Sparse Core Ops, SparseCore 0:
  176.3 172.3 all-reduce.2

commit v2 on v1

--- a/solution.py
+++ b/solution.py
@@ -466,12 +466,6 @@
     )(cotangent, *saved_vals, *consts)
 
 
-def weight_grad(operand, gradient):
-    a = operand.reshape(-1, operand.shape[-1])
-    b = gradient.reshape(-1, gradient.shape[-1])
-    return lax.dot_general(a, b, (((0,), (0,)), ((), ())), preferred_element_type=F32)
-
-
 def local_grads(tokens, resets, cotangent, stacked):
     weights = tuple(w if w.ndim == 2 else w[0] for w in stacked)
     rows, seq, width = tokens.shape
@@ -509,14 +503,429 @@
         weights,
         chunk,
     )
-    large = (
-        weight_grad(normed, g_gate),
-        weight_grad(normed, g_cand),
-        weight_grad(state_low, g_mix),
-        weight_grad(normed_two, g_up),
-        weight_grad(active, g_down),
+    operands = (active, g_down, g_up, normed_two, g_gate, normed, g_cand, state_low, g_mix)
+    return block_out, grad_in, operands, jnp.sum(small, axis=0)
+
+
+class Ring:
+    def __init__(self):
+        dp_size = lax.axis_size("dp")
+        rep_size = lax.axis_size("rep")
+        chips = dp_size // 2
+        self.inner = 4 if chips % 4 == 0 else chips
+        self.size = self.inner * rep_size
+        dp = lax.axis_index("dp")
+        self.rep = lax.axis_index("rep")
+        self.core = dp % 2
+        self.base = (dp // 2) // self.inner * self.inner
+        self.spot = (dp // 2) % self.inner
+        self.at = self.rep * self.inner + jnp.where(
+            self.rep % 2 == 0, self.spot, self.inner - 1 - self.spot
+        )
+        self.rep_size = rep_size
+
+    def device(self, place):
+        rep = place // self.inner
+        spot = place % self.inner
+        spot = jnp.where(rep % 2 == 0, spot, self.inner - 1 - spot)
+        return {"dp": (self.base + spot) * 2 + self.core, "rep": rep}
+
+    def next(self, direction):
+        step = 1 if direction == 0 else self.size - 1
+        return self.device((self.at + step) % self.size)
+
+    def shard(self, direction, back):
+        step = self.size - back if direction == 0 else back
+        return (self.at + step) % self.size
+
+    def other_core(self):
+        return {"dp": (self.base + self.spot) * 2 + 1 - self.core}
+
+    def doubling(self):
+        found = [self.other_core()]
+        span = 1
+        while span < self.inner:
+            flip = self.spot + span - 2 * span * ((self.spot // span) % 2)
+            found.append({"dp": (self.base + flip) * 2 + self.core})
+            span *= 2
+        span = 1
+        while span < self.rep_size:
+            found.append({"rep": self.rep + span - 2 * span * ((self.rep // span) % 2)})
+            span *= 2
+        return found
+
+
+def remote(src, dst, send_sem, recv_sem, device):
+    return pltpu.make_async_remote_copy(
+        src_ref=src,
+        dst_ref=dst,
+        send_sem=send_sem,
+        recv_sem=recv_sem,
+        device_id=device,
+        device_id_type=pl.DeviceIdType.MESH,
     )
-    return block_out, grad_in, large, jnp.sum(small, axis=0)
+
+
+def sum_kernel(
+    ring_size,
+    rounds,
+    active,
+    down,
+    up,
+    normed_two,
+    gate,
+    normed,
+    cand,
+    state,
+    mix,
+    small,
+    out,
+    small_out,
+    wide,
+    narrow,
+    turned,
+    own,
+    leave,
+    core_in,
+    first,
+    partial,
+    result,
+    small_buf,
+    wide_sem,
+    narrow_sem,
+    core_sem,
+    rs_send,
+    rs_recv,
+    ag_send,
+    ag_recv,
+    keep_sem,
+    pair_sem,
+    small_sem,
+):
+    ring = Ring()
+    width = down.shape[1]
+    groups = out.shape[0]
+    half_rows = out.shape[2]
+    side_rows = half_rows // 2
+    block = side_rows // ring_size
+    core = ring.core
+    away = 1 - core
+    pair = ring.other_core()
+    following = [ring.next(0), ring.next(1)]
+    doubling = ring.doubling()
+
+    barrier = pltpu.get_barrier_semaphore()
+    peers = following + doubling
+    for peer in peers:
+        pl.semaphore_signal(
+            barrier, inc=1, device_id=peer, device_id_type=pl.DeviceIdType.MESH
+        )
+
+    sources = [(active, down), (up, normed_two), (gate, normed), (None, mix)]
+
+    def wide_copy(g, half, t):
+        slot = g % 2
+        to = wide.at[slot, t, half]
+        if g < 3:
+            cols = pl.ds(pl.multiple_of((half * 2 + t) * width, width), width)
+            src = sources[g][0].at[:, cols]
+        else:
+            cols = pl.ds(pl.multiple_of(half * width, width), width)
+            src = (cand, state)[t].at[:, cols]
+        return pltpu.make_async_copy(src, to, wide_sem.at[slot, t, half])
+
+    def narrow_copy(g):
+        return pltpu.make_async_copy(
+            sources[g][1], narrow.at[g % 2], narrow_sem.at[g % 2]
+        )
+
+    def load(g):
+        narrow_copy(g).start()
+        for half in (away, core):
+            for t in range(2):
+                wide_copy(g, half, t).start()
+
+    def rows_of(direction, shard):
+        return pl.ds(pl.multiple_of(direction * side_rows + shard * block, block), block)
+
+    def core_copy(g, direction):
+        rows = pl.ds(direction * side_rows, side_rows)
+        return remote(
+            leave.at[g, rows],
+            core_in.at[g, rows],
+            core_sem.at[0, g, direction],
+            core_sem.at[1, g, direction],
+            pair,
+        )
+
+    def rs_copy(g, direction, k):
+        src = first.at[g, direction] if k == 0 else partial.at[g, direction, k - 1]
+        return remote(
+            src,
+            partial.at[g, direction, k],
+            rs_send.at[g, direction],
+            rs_recv.at[g, direction, k],
+            following[direction],
+        )
+
+    def ag_copy(g, direction, k):
+        rows = rows_of(direction, ring.shard(direction, k))
+        return remote(
+            result.at[g, rows],
+            result.at[g, rows],
+            ag_send.at[g, direction],
+            ag_recv.at[g, direction, k],
+            following[direction],
+        )
+
+    def hand_out(g, direction, k):
+        rows = rows_of(direction, ring.shard(direction, k))
+        pltpu.make_async_copy(
+            result.at[g, rows], out.at[g, core, rows], keep_sem.at[g, direction]
+        ).start()
+        remote(
+            result.at[g, rows],
+            out.at[g, core, rows],
+            pair_sem.at[0, g, direction],
+            pair_sem.at[1, g, direction],
+            pair,
+        ).start()
+
+    def mine(g, rows):
+        return own[g, rows, :] + core_in[g, rows, :].astype(F32)
+
+    last = ring_size - 1
+
+    def advance(g, stage):
+        for direction in range(2):
+            if stage == 0:
+                core_copy(g, direction).wait_recv()
+                rows = rows_of(direction, ring.shard(direction, 1))
+                first[g, direction] = mine(g, rows).astype(BF16)
+                rs_copy(g, direction, 0).start()
+            elif stage <= last:
+                k = stage - 1
+                rs_copy(g, direction, k).wait_recv()
+                rows = rows_of(direction, ring.shard(direction, k + 2))
+                total = partial[g, direction, k].astype(F32) + mine(g, rows)
+                if k < last - 1:
+                    partial[g, direction, k] = total.astype(BF16)
+                    rs_copy(g, direction, k + 1).start()
+                else:
+                    result[g, rows, :] = total.astype(BF16)
+                    ag_copy(g, direction, 0).start()
+                    hand_out(g, direction, 0)
+            else:
+                k = stage - last - 1
+                rows = rows_of(direction, ring.shard(direction, k + 1))
+                remote(
+                    result.at[g, rows],
+                    result.at[g, rows],
+                    ag_send.at[g, direction],
+                    ag_recv.at[g, direction, k],
+                    following[direction],
+                ).wait_recv()
+                if k < last - 1:
+                    ag_copy(g, direction, k + 1).start()
+                hand_out(g, direction, k + 1)
+
+    def small_copy(k):
+        return remote(
+            small_buf.at[0, k],
+            small_buf.at[1, k],
+            small_sem.at[0, k],
+            small_sem.at[1, k],
+            doubling[k],
+        )
+
+    def small_round(k):
+        if k == 0:
+            total = small[...]
+        else:
+            small_copy(k - 1).wait()
+            total = small_buf[0, k - 1] + small_buf[1, k - 1]
+        if k < rounds:
+            small_buf[0, k] = total
+            small_copy(k).start()
+        else:
+            small_out[...] = total
+
+    stages = 2 * last + 1
+    progress = [0] * groups
+    small_at = 0
+
+    load(0)
+    for g in range(groups):
+        if g + 1 < groups:
+            load(g + 1)
+        narrow_copy(g).wait()
+        turned[g % 2] = narrow[g % 2].T
+        for half in (away, core):
+            for t in range(2):
+                wide_copy(g, half, t).wait()
+                left = turned[(g if g < 3 or t == 1 else 2) % 2]
+                tile = dot(left, wide[g % 2, t, half])
+                if g == 0 or (g == 3 and t == 1):
+                    tile = tile.T
+                rows = pl.ds(t * width, width)
+                if half is away:
+                    leave[g, rows, :] = tile.astype(BF16)
+                else:
+                    own[g, rows, :] = tile
+            if half is away:
+                if g == 0:
+                    pl.semaphore_wait(barrier, len(peers))
+                for direction in range(2):
+                    core_copy(g, direction).start()
+            if small_at <= rounds:
+                small_round(small_at)
+                small_at += 1
+            for k in range(g):
+                advance(k, progress[k])
+                progress[k] += 1
+    while min(progress) < stages:
+        behind = sorted((k for k in range(groups) if progress[k] < stages), key=lambda k: progress[k])
+        for k in behind[:3]:
+            advance(k, progress[k])
+            progress[k] += 1
+        if small_at <= rounds:
+            small_round(small_at)
+            small_at += 1
+    while small_at <= rounds:
+        small_round(small_at)
+        small_at += 1
+
+    for g in range(groups):
+        for direction in range(2):
+            rows = pl.ds(direction * side_rows, side_rows)
+            core_copy(g, direction).wait_send()
+            sent = partial.at[g, direction]
+            remote(sent, sent, rs_send.at[g, direction], rs_recv.at[g, direction, 0], pair).wait_send()
+            sent = result.at[g, pl.ds(direction * side_rows, last * block)]
+            remote(sent, sent, ag_send.at[g, direction], ag_recv.at[g, direction, 0], pair).wait_send()
+            pltpu.make_async_copy(
+                result.at[g, rows], out.at[g, core, rows], keep_sem.at[g, direction]
+            ).wait()
+            whole_side = remote(
+                result.at[g, rows],
+                out.at[g, away, rows],
+                pair_sem.at[0, g, direction],
+                pair_sem.at[1, g, direction],
+                pair,
+            )
+            whole_side.wait_send()
+            whole_side.wait_recv()
+
+
+def unpack_kernel(down_i, up_i, gate_i, cand_i, out_i, w_gate, w_cand, w_out, w_up, w_down):
+    for source, target in (
+        (down_i, w_down),
+        (up_i, w_up),
+        (gate_i, w_gate),
+        (cand_i, w_cand),
+        (out_i, w_out),
+    ):
+        target[0] = source[0].astype(F32)
+
+
+def unpack(packed, width, hidden, ff):
+    packed = packed.reshape(4, ff, width)
+    parts = 8
+    tall = ff // parts
+    short = tall // 2
+    spread = width // tall
+    per_tile = width // short
+
+    def column_block(t):
+        return (0, t % spread, t // spread)
+
+    return pl.pallas_call(
+        unpack_kernel,
+        grid=(parts,),
+        out_shape=[
+            jax.ShapeDtypeStruct((1, width, 2 * hidden), F32),
+            jax.ShapeDtypeStruct((1, width, hidden), F32),
+            jax.ShapeDtypeStruct((1, hidden, width), F32),
+            jax.ShapeDtypeStruct((1, width, ff), F32),
+            jax.ShapeDtypeStruct((1, ff, width), F32),
+        ],
+        in_specs=[
+            pl.BlockSpec((1, tall, width), lambda t: (0, t, 0)),
+            pl.BlockSpec((1, tall, width), lambda t: (1, t, 0)),
+            pl.BlockSpec((1, tall, width), lambda t: (2, t, 0)),
+            pl.BlockSpec(
+                (1, short, width),
+                lambda t: (3, t // per_tile * 2 * per_tile + t % per_tile, 0),
+            ),
+            pl.BlockSpec(
+                (1, short, width),
+                lambda t: (3, t // per_tile * 2 * per_tile + per_tile + t % per_tile, 0),
+            ),
+        ],
+        out_specs=[
+            pl.BlockSpec((1, tall, width), column_block),
+            pl.BlockSpec((1, short, width), lambda t: (0, t % per_tile, t // per_tile)),
+            pl.BlockSpec((1, short, width), lambda t: (0, t, 0)),
+            pl.BlockSpec((1, tall, width), column_block),
+            pl.BlockSpec((1, tall, width), lambda t: (0, t, 0)),
+        ],
+        name="unpack",
+    )(packed, packed, packed, packed, packed)
+
+
+def sum_gradients(operands, small, hidden, ff):
+    ring = Ring()
+    n = ring.size
+    rounds = len(ring.doubling())
+    operands = [a.reshape(-1, a.shape[-1]) for a in operands]
+    tokens, width = operands[1].shape
+    groups = 4
+    half_rows = ff // 2
+    side_rows = half_rows // 2
+    block = side_rows // n
+    anywhere = pl.BlockSpec(memory_space=pl.ANY)
+    here = pl.BlockSpec(memory_space=pltpu.VMEM)
+    packed, small_sum = pl.pallas_call(
+        functools.partial(sum_kernel, n, rounds),
+        out_shape=[
+            jax.ShapeDtypeStruct((groups, 2, half_rows, width), BF16),
+            jax.ShapeDtypeStruct(small.shape, F32),
+        ],
+        in_specs=[anywhere] * 9 + [here],
+        out_specs=[anywhere, here],
+        scratch_shapes=[
+            pltpu.VMEM((2, 2, 2, tokens, width), BF16),
+            pltpu.VMEM((2, tokens, width), BF16),
+            pltpu.VMEM((2, width, tokens), BF16),
+            pltpu.VMEM((groups, half_rows, width), F32),
+            pltpu.VMEM((groups, half_rows, width), BF16),
+            pltpu.VMEM((groups, half_rows, width), BF16),
+            pltpu.VMEM((groups, 2, block, width), BF16),
+            pltpu.VMEM((groups, 2, n - 1, block, width), BF16),
+            pltpu.VMEM((groups, half_rows, width), BF16),
+            pltpu.VMEM((2, rounds) + small.shape, F32),
+            pltpu.SemaphoreType.DMA((2, 2, 2)),
+            pltpu.SemaphoreType.DMA((2,)),
+            pltpu.SemaphoreType.DMA((2, groups, 2)),
+            pltpu.SemaphoreType.DMA((groups, 2)),
+            pltpu.SemaphoreType.DMA((groups, 2, n - 1)),
+            pltpu.SemaphoreType.DMA((groups, 2)),
+            pltpu.SemaphoreType.DMA((groups, 2, n - 1)),
+            pltpu.SemaphoreType.DMA((groups, 2)),
+            pltpu.SemaphoreType.DMA((2, groups, 2)),
+            pltpu.SemaphoreType.DMA((2, rounds)),
+        ],
+        compiler_params=pltpu.CompilerParams(
+            collective_id=2, has_side_effects=True, vmem_limit_bytes=VMEM_LIMIT
+        ),
+        name="sum_gradients",
+    )(*operands, small)
+    dp_size = lax.axis_size("dp")
+    inner = 2 * ring.inner
+    if dp_size > inner:
+        members = [list(range(i, dp_size, inner)) for i in range(inner)]
+        packed, small_sum = lax.psum((packed, small_sum), "dp", axis_index_groups=members)
+    return unpack(packed, width, hidden, ff), small_sum
 
 
 def split_small(small, width, hidden, ff):
@@ -530,15 +939,17 @@
 
 
 def body(tokens, resets, cotangent, *stacked):
-    block_out, grad_in, large, small = local_grads(tokens, resets, cotangent, stacked)
+    block_out, grad_in, operands, small = local_grads(tokens, resets, cotangent, stacked)
     width = tokens.shape[2]
     hidden = stacked[3].shape[2]
     ff = stacked[8].shape[2]
-    sums = lax.psum(tuple(g.astype(BF16) for g in large) + (small,), ("dp", "rep"))
-    w_gate, w_cand, w_out, w_up, w_down = (s.astype(F32) for s in sums[:5])
-    g_one, b_gate, b_cand, b_out, g_two, b_up, b_down = split_small(sums[5], width, hidden, ff)
+    large, small_sum = sum_gradients(operands, small.reshape(LANES, -1), hidden, ff)
+    w_gate, w_cand, w_out, w_up, w_down = large
+    g_one, b_gate, b_cand, b_out, g_two, b_up, b_down = split_small(
+        small_sum.reshape(-1), width, hidden, ff
+    )
     grads = (g_one, w_gate, b_gate, w_cand, b_cand, w_out, b_out, g_two, w_up, b_up, w_down, b_down)
-    return (block_out, grad_in) + tuple(g[None] for g in grads)
+    return (block_out, grad_in) + tuple(g if g.ndim == 3 else g[None] for g in grads)
 
 
 def solution(mesh):

time: 374 us -> 267 us (0.71)
  Pallas kernels: 136 us -> 253 us
  waiting for transfers between devices: 106 us -> 0 us
  blocking collectives: 63.4 us -> 0 us
  matrix products: 29.9 us -> 0 us
  between operations: 14.2 us -> 0.72 us
  other arithmetic: 14.3 us -> 2.67 us
    pallas_call x0 -> x2, Pallas kernels: none -> 118 us  [the longest x1 108 us: sum_gradients(): pl.pallas_call(functools.partial(sum_kernel, n, rounds), out_shape=[jax.S...]
    psum x1 -> x0, waiting for transfers between devices: 106 us -> none  [body(): lax.psum(tuple((g.astype(BF16) for g in large)) + (small,), ('dp', 'rep'))]
    psum x1 -> x0, blocking collectives: 63.4 us -> none  [body(): lax.psum(tuple((g.astype(BF16) for g in large)) + (small,), ('dp', 'rep'))]
    dot_general x5 -> x0, matrix products: 29.9 us -> none  [weight_grad(): lax.dot_general(a, b, (((0,), (0,)), ((), ())), preferred_element_type=F32)]
    broadcast_in_dim x5 -> x0, other arithmetic: 12.5 us -> none  [body(): return (block_out, grad_in) + tuple((g[None] for g in grads))]
  transfers between devices with their start and end apart: 1 -> 0, of which waited for: 1 -> 0; matrix products, arithmetic and copies ran while one was open for 0% -> 0% of each run, Pallas kernels for 0% -> 0%
where the time goes in v2:
time: 267 us; the launch traced here: 266 us
  Pallas kernels  253 us (95%)
  local copies, waits for them, and re-layouts  9.69 us (4%)
  other arithmetic  2.67 us (1%)
    pallas_call x1, Pallas kernels, sum_gradients(): pl.pallas_call(functools.partial(sum_kernel, n, rounds), out_shape=[jax.S...  108 us
    pallas_call x1, Pallas kernels, run_backward(): pl.pallas_call(functools.partial(backward_kernel, steps, LANES // rows),...  71.7 us
    pallas_call x1, Pallas kernels, run_forward(): pl.pallas_call(functools.partial(forward_kernel, steps, LANES // rows), g...  63.5 us
    pallas_call x1, Pallas kernels, unpack(): pl.pallas_call(unpack_kernel, grid=(parts,), out_shape=[jax.ShapeDtypeStr...  10.1 us

profile of v2, /device:TPU:0, one launch (start us, length us, event | category | flops | bytes accessed | tf_op | source)
XLA Modules:
  0.0 266.0 jit_solution(17832210676389580091)
XLA Ops:
  0.7 0.7 subtract_convert_fusion
  1.4 0.1 reshape.69
  1.5 0.1 copy.30
  1.6 0.1 copy.31
  1.7 0.9 fusion.1
  2.6 1.3 broadcast_in_dim.29.keep
  3.9 63.5 %forward_block.1 = (bf16[1,2,1024,512]{3,2,1,0:T(8,128)(2,1)}, bf16[8,256,512]{2,1,0:T(8,128)(2,1)}, bf16[8,256,512]{2,1,0:T(8,128)(2,1)}, f32[8,256,1024]{2,1,0...) custom-call(bf16[2,1024,512]{2,1,0:T(8,128)(2,1)} %tok.1, ...), custom_call_target="tpu_custom_call" | custom-call | tf_op jit(solution)/shard_map/forward_block/pallas_call | solution.py:389
  67.4 71.7 %backward_block.1 = (f32[1,2,1024,512]{3,2,1,0:T(8,128)}, bf16[8,256,512]{2,1,0:T(8,128)(2,1)}, bf16[8,256,2048]{2,1,0:T(8,128)(2,1)}, bf16[8,256,512]{2,1,0:T(8...) custom-call(bf16[2,1024,512]{2,1,0:T(8,128)(2,1)} %cot.1, ...), custom_call_target="tpu_custom_call" | custom-call | tf_op jit(solution)/shard_map/backward_block/pallas_call | solution.py:447
  139.1 1.0 reduce_sum.9
  140.1 0.6 reshape.79.small
  140.7 107.6 %sum_gradients.1 = (bf16[4,2,1024,512]{3,2,1,0:T(8,128)(2,1)}, f32[8,896]{1,0:T(8,128)}) custom-call(bf16[2048,2048]{1,0:T(8,128)(2,1)} %bitcast.36, bf16[2048,512]{1,0:T(8,128)(2,1)} %bitcast.47, bf16[2048,2048]{1,0:T(8,128)(2,1)} %bitcast.37, bf16[2048,512]{1,0:T(8,128)(2,1)} %bitcast.46, bf16[2048,2048]{1,0:T(8,128)(2,1)} %bitcast.38, ...), custom_call_target="tpu_custom_call" | custom-call | tf_op jit(solution)/shard_map/sum_gradients/pallas_call | solution.py:888
  248.4 0.8 reshape.80
  249.1 0.6 slice.30
  249.7 0.6 fusion.4
  250.3 0.6 fusion.5
  250.9 0.0 copy-start.1
  250.9 10.1 %unpack.1 = (f32[1,512,2048]{2,1,0:T(8,128)}, f32[1,512,1024]{2,1,0:T(8,128)}, f32[1,1024,512]{2,1,0:T(8,128)}, f32[1,512,2048]{2,1,0:T(8,128)}, f32[1,2048,512]{2,1,0:T(8,128)}) custom-call(bf16[4,2048,512]{2,1,0:T(8,128)(2,1)} %bitcast.25, bf16[4,2048,512]{2,1,0:T(8,128)(2,1)} %bitcast.26, bf16[4,2048,512]{2,1,0:T(8,128)(2,1)} %bitcast.27, ...), custom_call_target="tpu_custom_call" | custom-call | tf_op jit(solution)/shard_map/unpack/pallas_call | solution.py:842
  261.1 0.0 copy-start
  261.1 0.0 copy-done.1
  261.1 1.3 copy.34
  262.4 1.6 copy-done
  264.0 2.0 copy.35
  (3 shorter events, 0.0 us)
Async XLA Ops:
  250.9 10.2 %copy-start.1 = (bf16[1,2,1024,512]{3,2,1,0:T(8,128)(2,1)S(1)}, bf16[1,2,1024,512]{3,2,1,0:T(8,128)(2,1)}, u32[]{:S(2)}) copy-start(bf16[1,2,1024,512]{3,2,1,0:T(8,128)(2,1)} %get-tuple-element.94) | copy-start | bytes 6291460
  261.1 2.9 %copy-start = (f32[1,2,1024,512]{3,2,1,0:T(8,128)S(1)}, f32[1,2,1024,512]{3,2,1,0:T(8,128)}, u32[]{:S(2)}) copy-start(f32[1,2,1024,512]{3,2,1,0:T(8,128)} %get-tuple-element.95) | copy-start | bytes 12582916

commit v3 on v1

v3 whole, which is shorter than its diff:
```python
import functools
import math

import jax
import jax.numpy as jnp
from jax import lax
from jax.experimental import pallas as pl
from jax.experimental.pallas import tpu as pltpu
from jax.sharding import PartitionSpec as P

EPS = 1e-06
F32 = jnp.float32
BF16 = jnp.bfloat16
CHUNK = 256
LANES = 8
WIDTH = 256
GELU_A = math.sqrt(2.0 / math.pi)
GELU_B = 0.044715
LN4 = math.log(4.0)
EXP_TOP = 85.6
VMEM_LIMIT = 60 * 1024 * 1024
BLOCKS_VMEM = 63 * 1024 * 1024


def dot(a, b):
    return jnp.dot(a, b, preferred_element_type=F32)


def dot_nt(a, b):
    return lax.dot_general(a, b, (((1,), (1,)), ((), ())), preferred_element_type=F32)


def inv_scale(values):
    return lax.rsqrt(jnp.mean(values * values, axis=-1, keepdims=True) + EPS)


def partner_barrier_signal(partner):
    pl.semaphore_signal(
        pltpu.get_barrier_semaphore(),
        inc=1,
        device_id={"section": partner},
        device_id_type=pl.DeviceIdType.MESH,
    )


def interleave(*streams):
    live = list(streams)
    while live:
        for stream in list(live):
            if next(stream, live) is live:
                live.remove(stream)


def scan_segments(product, accum, carry, reverse):
    which = lax.broadcasted_iota(jnp.int32, product.shape, 0)
    span = 1
    while span < LANES:
        turn = LANES - span if reverse else span
        inside = which < LANES - span if reverse else which >= span
        accum = jnp.where(inside, product * pltpu.roll(accum, turn, 0) + accum, accum)
        product = jnp.where(inside, product * pltpu.roll(product, turn, 0), product)
        span *= 2
    reached = product * carry + accum
    edge = LANES - 1 if reverse else 0
    incoming = jnp.where(which == edge, carry, pltpu.roll(reached, LANES - 1 if reverse else 1, 0))
    end = 0 if reverse else LANES - 1
    return incoming, jnp.broadcast_to(reached[end : end + 1], reached.shape)


class Step:
    def __init__(self, step, rows, chunks):
        first = lax.axis_index("section") == 0
        phase = step // (chunks + 1)
        self.at = step % (chunks + 1)
        self.forward = jnp.where(first, phase < rows, phase % 2 == 0)
        self.row = jnp.where(first, phase % rows, phase // 2)
        base = self.row * chunks
        last = chunks - 1
        before = jnp.where(first, last, jnp.maximum(base - chunks, jnp.where(self.row == 0, last, 0)))
        after = jnp.where(first, rows * chunks - 1, base + last)
        self.mixer = jnp.where(self.forward, base + jnp.minimum(self.at, last), after)
        self.feed = jnp.where(self.forward, base + jnp.maximum(self.at - 1, 0), after)
        self.back_feed = jnp.where(self.forward, before, base + jnp.maximum(last - self.at, 0))
        self.back_mixer = jnp.where(self.forward, before, base + jnp.minimum(chunks - self.at, last))
        self.next_mixer = jnp.minimum(self.mixer + 1, rows * chunks - 1)
        later = jnp.minimum(base + self.at + 1, rows * chunks - 1)
        later = jnp.where(self.forward, base, jnp.minimum(later, base + chunks))
        later = jnp.minimum(later, rows * chunks - 1)
        self.next_back = later // chunks * chunks + last - later % chunks


def blocks_kernel(
    rows,
    chunks,
    first_tok,
    tok,
    first_cot,
    cot,
    keep,
    perm,
    g_one,
    w_gate,
    b_gate,
    w_cand,
    b_cand,
    w_out,
    b_out,
    g_two,
    w_up,
    b_up,
    w_down,
    b_down,
    operands_o,
    active_o,
    low_o,
    down_o,
    up_o,
    mix_o,
    gate_o,
    cand_o,
    grad_in,
    small_o,
    ratio_s,
    slopes_s,
    middle_s,
    slope_up_s,
    inputs,
    send,
    received,
    coming,
    coming_back,
    carry,
    carry_back,
    normed_two_s,
    grad_middle_s,
    mix_s,
    send_sem,
    input_sem,
    back_send_sem,
    received_sem,
):
    c = pl.program_id(0)
    section = lax.axis_index("section")
    partner = 1 - section
    step = Step(c, rows, chunks)
    _, tokens, width = tok.shape
    hidden = w_cand.shape[1]
    ff = w_up.shape[1]
    span = tokens // LANES
    total = rows * chunks
    final = 2 * rows * (chunks + 1) - 1

    def chunk_copy(slot):
        return remote(
            send.at[slot],
            inputs.at[slot],
            send_sem.at[slot],
            input_sem.at[slot],
            {"section": partner},
        )

    def back_copy(slot):
        return remote(
            send.at[slot],
            received.at[slot],
            back_send_sem.at[slot],
            received_sem.at[slot],
            {"section": partner},
        )

    def add_small(which, values):
        part = jnp.sum(values.reshape(-1, LANES, width), axis=0)
        small_o[:, which * width : (which + 1) * width] += part

    @pl.when(c == 0)
    def _():
        partner_barrier_signal(partner)
        small_o[...] = jnp.zeros_like(small_o)
        coming[...] = dot(perm[...], first_tok[0]).astype(BF16)
        coming_back[...] = dot(perm[...], first_cot[0]).astype(BF16)
        pl.semaphore_wait(pltpu.get_barrier_semaphore(), 1)

    @pl.when(step.forward & (step.at == 0))
    def _():
        carry[...] = jnp.zeros_like(carry)

    @pl.when(jnp.logical_not(step.forward) & (step.at == 0))
    def _():
        carry_back[...] = jnp.zeros_like(carry_back)

    @pl.when(step.forward & (step.at < chunks) & (section == 0))
    def _():
        inputs[step.mixer] = coming[...]

    @pl.when(step.forward & (step.at < chunks) & (section == 1))
    def _():
        chunk_copy(step.mixer).wait_recv()

    @pl.when(jnp.logical_not(step.forward) & (step.at < chunks) & (section == 0))
    def _():
        back_copy(step.back_feed).wait_recv()
        coming_back[...] = received[step.back_feed]

    def mixer():
        at_chunk = step.mixer
        x = inputs[at_chunk].astype(F32)
        normed = (x * inv_scale(x) * g_one[...]).astype(BF16)
        operands_o[0, :, :width] = normed
        yield
        for at in range(0, hidden, WIDTH):
            cols = slice(at, at + WIDTH)
            cols_in = slice(hidden + at, hidden + at + WIDTH)
            pre_f = dot(normed, w_gate[:, cols])
            pre_i = dot(normed, w_gate[:, cols_in])
            cand = dot(normed, w_cand[:, cols]) + b_cand[:, cols]
            u = jnp.exp(jnp.minimum((-LN4 - b_gate[:, cols]) - pre_f, EXP_TOP))
            v = jnp.exp(jnp.minimum((-LN4 - b_gate[:, cols_in]) - pre_i, EXP_TOP))
            d = 1.0 / (0.5 + u + v)
            ratio_f = (0.25 + v) * d
            ratio_i = (0.25 + u) * d
            ratio_s[at_chunk, :, cols] = ratio_f
            keep_w = jnp.concatenate([keep[0]] * (WIDTH // 128), axis=1)
            decay = ratio_f * keep_w
            drive = ratio_i * cand
            product = decay[0:LANES]
            accum = drive[0:LANES]
            for j in range(1, span):
                r = slice(j * LANES, (j + 1) * LANES)
                accum = decay[r] * accum + drive[r]
                product = decay[r] * product
            state, carry[:, cols] = scan_segments(product, accum, carry[:, cols], False)
            before = []
            after = []
            for j in range(span):
                r = slice(j * LANES, (j + 1) * LANES)
                before.append(state)
                state = decay[r] * state + drive[r]
                after.append(state)
            operands_o[0, :, width + at : width + at + WIDTH] = jnp.concatenate(
                after, axis=0
            ).astype(BF16)
            lever = keep_w * jnp.concatenate(before, axis=0) - cand
            slopes_s[at_chunk, :, cols] = (lever * ((u * d) * ratio_f)).astype(BF16)
            slopes_s[at_chunk, :, cols_in] = (-lever * ((v * d) * ratio_i)).astype(BF16)
            yield
        mixed = dot(operands_o[0, :, width : width + hidden], w_out[...])
        yield
        middle = x + (mixed + b_out[...])
        normed_two = (middle * inv_scale(middle) * g_two[...]).astype(BF16)
        operands_o[0, :, width + hidden :] = normed_two
        yield
        middle_s[at_chunk] = middle
        normed_two_s[...] = normed_two

    def feed():
        at_chunk = step.feed
        for at in range(0, ff, WIDTH):
            cols = slice(at, at + WIDTH)
            up = dot(normed_two_s[...], w_up[:, cols]) + b_up[:, cols]
            square = up * up
            half = 0.5 + 0.5 * jnp.tanh(up * (GELU_A + (GELU_A * GELU_B) * square))
            act = up * half
            active_o[0, :, cols] = act.astype(BF16)
            slope = half + act * (1.0 - half) * (2 * GELU_A + (6 * GELU_A * GELU_B) * square)
            slope_up_s[at_chunk, :, cols] = slope.astype(BF16)
            if at % (2 * WIDTH):
                yield
        down = dot(active_o[0], w_down[...])
        yield
        low_o[0] = (middle_s[at_chunk] + (down + b_down[...])).astype(BF16)

    def reorder():
        yield
        yield
        coming[...] = dot(perm[...], tok[0]).astype(BF16)

    def back_feed():
        at_chunk = step.back_feed
        grad_down = coming_back[...]
        down_o[0] = grad_down
        yield
        for at in range(0, ff, WIDTH):
            cols = slice(at, at + WIDTH)
            grad_active = dot_nt(grad_down, w_down[cols, :])
            slope = slope_up_s[at_chunk, :, cols].astype(F32)
            up_o[0, :, cols] = (grad_active * slope).astype(BF16)
            if at % (2 * WIDTH):
                yield
        q = dot_nt(up_o[0], w_up[...])
        yield
        dy = grad_down.astype(F32)
        add_small(3, dy)
        middle = middle_s[at_chunk]
        r = inv_scale(middle)
        scaled = middle * r
        add_small(2, q * scaled)
        weighted = q * g_two[...]
        grad_middle = dy + r * (
            weighted - scaled * jnp.mean(weighted * scaled, axis=-1, keepdims=True)
        )
        add_small(1, grad_middle)
        grad_mix = grad_middle.astype(BF16)
        mix_o[0] = grad_mix
        yield
        yield
        grad_middle_s[...] = grad_middle
        mix_s[...] = grad_mix

    def back_mixer():
        at_chunk = step.back_mixer
        for at in range(0, hidden, WIDTH):
            cols = slice(at, at + WIDTH)
            cols_in = slice(hidden + at, hidden + at + WIDTH)
            grad_state = dot_nt(mix_s[...], w_out[cols, :])
            ratio_f = ratio_s[at_chunk, :, cols]
            decay = ratio_f * jnp.concatenate([keep[0]] * (WIDTH // 128), axis=1)
            last = slice((span - 1) * LANES, span * LANES)
            product = decay[last]
            accum = decay[last] * grad_state[last]
            for j in range(span - 2, -1, -1):
                rj = slice(j * LANES, (j + 1) * LANES)
                accum = decay[rj] * (grad_state[rj] + accum)
                product = decay[rj] * product
            later, carry_back[:, cols] = scan_segments(product, accum, carry_back[:, cols], True)
            parts = [None] * span
            for j in range(span - 1, -1, -1):
                rj = slice(j * LANES, (j + 1) * LANES)
                carried = grad_state[rj] + later
                parts[j] = carried
                later = decay[rj] * carried
            carried = jnp.concatenate(parts, axis=0)
            gate_o[0, :, cols] = (carried * slopes_s[at_chunk, :, cols].astype(F32)).astype(BF16)
            gate_o[0, :, cols_in] = (
                carried * slopes_s[at_chunk, :, cols_in].astype(F32)
            ).astype(BF16)
            cand_o[0, :, cols] = (carried * (1.0 - ratio_f)).astype(BF16)
            yield
        p = dot_nt(gate_o[0], w_gate[...]) + dot_nt(cand_o[0], w_cand[...])
        yield
        x = inputs[at_chunk].astype(F32)
        r = inv_scale(x)
        scaled = x * r
        add_small(0, p * scaled)
        weighted = p * g_one[...]
        grad_in[0] = grad_middle_s[...] + r * (
            weighted - scaled * jnp.mean(weighted * scaled, axis=-1, keepdims=True)
        )

    def back_reorder():
        yield
        yield
        coming_back[...] = dot(perm[...], cot[0]).astype(BF16)

    opening = step.at == 0
    closing = step.at == chunks
    between = jnp.logical_not(opening | closing)
    backward = jnp.logical_not(step.forward)

    @pl.when(step.forward & opening)
    def _():
        interleave(mixer(), reorder())

    @pl.when(step.forward & between)
    def _():
        interleave(mixer(), feed(), reorder())

    @pl.when(step.forward & closing)
    def _():
        interleave(feed())

    @pl.when(backward & opening)
    def _():
        interleave(back_feed(), back_reorder())

    @pl.when(backward & between)
    def _():
        interleave(back_feed(), back_mixer(), back_reorder())

    @pl.when(backward & closing)
    def _():
        interleave(back_mixer())

    @pl.when(step.forward & jnp.logical_not(opening) & (section == 0))
    def _():
        send[step.feed] = low_o[0]
        chunk_copy(step.feed).start()

    @pl.when(backward & jnp.logical_not(opening) & (section == 1))
    def _():
        send[step.back_mixer] = grad_in[0].astype(BF16)
        back_copy(step.back_mixer).start()

    @pl.when((c == final) & (section == 0))
    def _():
        for slot in range(total):
            chunk_copy(slot).wait_send()

    @pl.when((c == final) & (section == 1))
    def _():
        for slot in range(total):
            back_copy(slot).wait_send()


def whole(array):
    zeros = (0,) * array.ndim
    return pl.BlockSpec(array.shape, lambda c: zeros, pipeline_mode=pl.Buffered(1))


def run_blocks(tokens, cotangent, keep, perm, weights, chunk):
    rows, seq, width = tokens.shape
    chunks = seq // chunk
    total = rows * chunks
    hidden = weights[3].shape[1]
    ff = weights[8].shape[1]

    def index(name):
        def of_step(c):
            return (getattr(Step(c, rows, chunks), name), 0, 0)

        return of_step

    def rows_of(name):
        def of_step(c):
            at = getattr(Step(c, rows, chunks), name)
            return (at // chunks, at % chunks, 0)

        return of_step

    def keep_of(c):
        step = Step(c, rows, chunks)
        return (jnp.where(step.forward, step.mixer, step.back_mixer), 0, 0)

    def given(columns, dtype, name):
        shape = jax.ShapeDtypeStruct((total, chunk, columns), dtype)
        return shape, pl.BlockSpec((1, chunk, columns), index(name))

    outs = [
        given(2 * width + hidden, BF16, "mixer"),
        given(ff, BF16, "feed"),
        given(width, BF16, "feed"),
        given(width, BF16, "back_feed"),
        given(ff, BF16, "back_feed"),
        given(width, BF16, "back_feed"),
        given(2 * hidden, BF16, "back_mixer"),
        given(hidden, BF16, "back_mixer"),
        given(width, F32, "back_mixer"),
        (
            jax.ShapeDtypeStruct((LANES, 4 * width), F32),
            pl.BlockSpec((LANES, 4 * width), lambda c: (0, 0)),
        ),
    ]
    part = (1, chunk, width)
    once = pl.Buffered(1)
    return pl.pallas_call(
        functools.partial(blocks_kernel, rows, chunks),
        grid=(2 * rows * (chunks + 1),),
        out_shape=[o[0] for o in outs],
        in_specs=[
            pl.BlockSpec(part, lambda c: (0, 0, 0), pipeline_mode=once),
            pl.BlockSpec(part, rows_of("next_mixer")),
            pl.BlockSpec(part, lambda c: (0, chunks - 1, 0), pipeline_mode=once),
            pl.BlockSpec(part, rows_of("next_back")),
            pl.BlockSpec((1, chunk, 128), keep_of),
            whole(perm),
        ]
        + [whole(w) for w in weights],
        out_specs=[o[1] for o in outs],
        scratch_shapes=[
            pltpu.VMEM((total, chunk, hidden), F32),
            pltpu.VMEM((total, chunk, 2 * hidden), BF16),
            pltpu.VMEM((total, chunk, width), F32),
            pltpu.VMEM((total, chunk, ff), BF16),
            pltpu.VMEM((total, chunk, width), BF16),
            pltpu.VMEM((total, chunk, width), BF16),
            pltpu.VMEM((total, chunk, width), BF16),
            pltpu.VMEM((chunk, width), BF16),
            pltpu.VMEM((chunk, width), BF16),
            pltpu.VMEM((LANES, hidden), F32),
            pltpu.VMEM((LANES, hidden), F32),
            pltpu.VMEM((chunk, width), BF16),
            pltpu.VMEM((chunk, width), F32),
            pltpu.VMEM((chunk, width), BF16),
            pltpu.SemaphoreType.DMA((total,)),
            pltpu.SemaphoreType.DMA((total,)),
            pltpu.SemaphoreType.DMA((total,)),
            pltpu.SemaphoreType.DMA((total,)),
        ],
        compiler_params=pltpu.CompilerParams(
            collective_id=0, has_side_effects=True, vmem_limit_bytes=BLOCKS_VMEM
        ),
        name="blocks",
    )(tokens, tokens, cotangent, cotangent, keep, perm, *weights)


def local_grads(tokens, resets, cotangent, stacked):
    weights = tuple(w if w.ndim == 2 else w[0] for w in stacked)
    rows, seq, width = tokens.shape
    chunk = min(CHUNK, seq)
    total = rows * (seq // chunk)
    span = chunk // LANES
    keep = (1 - resets).astype(F32).reshape(total, LANES, span)
    keep = keep.transpose(0, 2, 1).reshape(total, chunk, 1)
    keep = jnp.broadcast_to(keep, (total, chunk, 128))
    at = lax.broadcasted_iota(jnp.int32, (chunk, chunk), 0)
    source = lax.broadcasted_iota(jnp.int32, (chunk, chunk), 1)
    perm = (source == (at % LANES) * span + at // LANES).astype(BF16)
    perm_t = (at == (source % LANES) * span + source // LANES).astype(BF16)
    operands, active, low, *grads, grad_in, small = run_blocks(
        tokens, cotangent, keep, perm, weights, chunk
    )
    return low, grad_in, perm_t, (operands, active, *grads, small)


class Place:
    def __init__(self):
        dp_size = lax.axis_size("dp")
        chips = dp_size // 2
        self.line = 4 if chips % 4 == 0 else chips
        dp = lax.axis_index("dp")
        self.side = lax.axis_index("rep")
        self.core = dp % 2
        self.base = (dp // 2) // self.line * self.line
        self.spot = (dp // 2) % self.line

    def along(self, step):
        return {"dp": (self.base + self.spot + step) * 2 + self.core}

    def across(self):
        return {"rep": 1 - self.side}

    def other_core(self):
        return {"dp": (self.base + self.spot) * 2 + 1 - self.core}

    def doubling(self):
        found = [self.other_core()]
        span = 1
        while span < self.line:
            found.append(self.along(span - 2 * span * ((self.spot // span) % 2)))
            span *= 2
        return found + [self.across()]


def remote(src, dst, send_sem, recv_sem, device):
    return pltpu.make_async_remote_copy(
        src_ref=src,
        dst_ref=dst,
        send_sem=send_sem,
        recv_sem=recv_sem,
        device_id=device,
        device_id_type=pl.DeviceIdType.MESH,
    )


SUM_ORDER = (
    -1, -1, 1, 0, -1, 1, -1, 3, 1, 2, 3, -1, 0, 3, 0, -1, 1, 5, 0, 3, 4, 2, 5, 1, 2, 0, -1, 3,
    2, 5, 0, 1, -1, 3, 7, 6, 4, 2, 5, 0, 4, 1, 7, 2, 4, 3, 6, 7, 2, 6, 4, 7, 6, 2, 3, 0, 4, 6,
    4, 1, 5, 6, 7, 6, 5, 2, 4, 7, 6, 4, 5, 7, 5, 0, 6, 7,
)


def sum_order(groups, lengths):
    if all(SUM_ORDER.count(c) == n for c, n in enumerate(lengths)):
        return SUM_ORDER
    order = []
    left = list(lengths)
    for g in range(groups):
        for _ in range(2):
            order.append(-1)
            for c in range(2 * g):
                if left[c]:
                    order.append(c)
                    left[c] -= 1
    while any(left):
        for c, n in enumerate(left):
            if n:
                order.append(c)
                left[c] -= 1
    return order


def sum_kernel(
    line,
    rounds,
    operands,
    feed,
    down,
    up,
    mix,
    gate,
    cand,
    small,
    out,
    small_out,
    wide,
    narrow,
    turned,
    own,
    leave,
    core_in,
    across_out,
    across_in,
    short_out,
    short_in,
    partial,
    result,
    small_buf,
    sums,
    wide_sem,
    narrow_sem,
    core_sem,
    across_sem,
    back_sem,
    short_sem,
    line_send,
    rs_recv,
    ag_recv,
    keep_sem,
    pair_sem,
    small_sem,
):
    place = Place()
    width = down.shape[1]
    groups = out.shape[0]
    half_rows = out.shape[2]
    last = line - 1
    side_rows = across_out.shape[1]
    shard_rows = (side_rows // line, short_out.shape[1])
    short_at = 2 * side_rows
    core = place.core
    away = 1 - core
    pair = place.other_core()
    opposite = place.across()
    neighbours = (place.along(1), place.along(-1))
    spots = (place.spot, last - place.spot)
    doubling = place.doubling()

    barrier = pltpu.get_barrier_semaphore()

    def greet(peer):
        pl.semaphore_signal(
            barrier, inc=1, device_id=peer, device_id_type=pl.DeviceIdType.MESH
        )

    for peer in doubling:
        greet(peer)
    for direction in range(2):
        pl.when(spots[direction] < last)(functools.partial(greet, neighbours[direction]))
    greeted = len(doubling) + jnp.where(spots[0] < last, 1, 0) + jnp.where(spots[1] < last, 1, 0)

    hidden = cand.shape[1]
    ff = up.shape[1]
    normed_two = operands.at[:, pl.ds(width + hidden, width)]
    normed = operands.at[:, pl.ds(0, width)]
    sources = [(feed, down), (up, normed_two), (gate, normed), (None, mix)]
    sum_at = [None, 0, ff, ff + 2 * hidden]

    def wide_copy(g, half, t):
        slot = g % 2
        to = wide.at[slot, t, half]
        if g < 3:
            cols = pl.ds(pl.multiple_of((half * 2 + t) * width, width), width)
            src = sources[g][0].at[:, cols]
        elif t == 0:
            cols = pl.ds(pl.multiple_of(half * width, width), width)
            src = cand.at[:, cols]
        else:
            cols = pl.ds(pl.multiple_of(width + half * width, width), width)
            src = operands.at[:, cols]
        return pltpu.make_async_copy(src, to, wide_sem.at[slot, t, half])

    def narrow_copy(g):
        return pltpu.make_async_copy(
            sources[g][1], narrow.at[g % 2], narrow_sem.at[g % 2]
        )

    def load(g):
        narrow_copy(g).start()
        for half in (away, core):
            for t in range(2):
                wide_copy(g, half, t).start()

    def side_at(side):
        return pl.ds(pl.multiple_of(side * side_rows, side_rows), side_rows)

    def shard_at(kind, shard):
        n = shard_rows[kind]
        start = place.side * side_rows if kind == 0 else short_at
        return pl.ds(pl.multiple_of(start + shard * n, 16), n)

    def core_copy(g, kind):
        rows = pl.ds(0, short_at) if kind == 0 else pl.ds(short_at, half_rows - short_at)
        return remote(
            leave.at[g, rows],
            core_in.at[g, rows],
            core_sem.at[0, g, kind],
            core_sem.at[1, g, kind],
            pair,
        )

    def rs_copy(g, kind, direction, source, s):
        rows = pl.ds(0, shard_rows[kind])
        return remote(
            partial.at[g, kind, direction, source, rows],
            partial.at[g, kind, direction, s, rows],
            line_send.at[g, kind, direction],
            rs_recv.at[g, kind, direction, s],
            neighbours[direction],
        )

    def ag_copy(g, kind, direction, shard, s):
        rows = shard_at(kind, shard)
        return remote(
            result.at[g, rows],
            result.at[g, rows],
            line_send.at[g, kind, direction],
            ag_recv.at[g, kind, direction, s],
            neighbours[direction],
        )

    def across_copy(g):
        return remote(
            across_out.at[g], across_in.at[g], across_sem.at[0, g], across_sem.at[1, g], opposite
        )

    def short_copy(g):
        return remote(
            short_out.at[g], short_in.at[g], short_sem.at[0, g], short_sem.at[1, g], opposite
        )

    def back_copy(g, rows):
        return remote(
            result.at[g, rows], result.at[g, rows], back_sem.at[0, g], back_sem.at[1, g], opposite
        )

    def keep_copy(g, rows):
        return pltpu.make_async_copy(result.at[g, rows], out.at[g, core, rows], keep_sem.at[g])

    def pair_copy(g, rows, to):
        return remote(
            result.at[g, rows], out.at[g, to, rows], pair_sem.at[0, g], pair_sem.at[1, g], pair
        )

    def hand_out(g, rows):
        keep_copy(g, rows).start()
        pair_copy(g, rows, core).start()

    def shard_of(direction, steps):
        return steps if direction == 0 else last - steps

    def rs_stage(g, kind, s):
        rows = pl.ds(0, shard_rows[kind])
        for direction in range(2):
            spot = spots[direction]
            mine = shard_at(kind, shard_of(direction, spot + last - s))

            def begin(direction=direction):
                first = shard_at(kind, shard_of(direction, last - s))
                partial[g, kind, direction, s, rows] = own[g, first].astype(BF16)
                rs_copy(g, kind, direction, s, s).start()

            def go_on(direction=direction, mine=mine):
                rs_copy(g, kind, direction, s - 1, s - 1).wait_recv()
                total = own[g, mine] + partial[g, kind, direction, s - 1, rows].astype(F32)
                partial[g, kind, direction, s - 1, rows] = total.astype(BF16)
                rs_copy(g, kind, direction, s - 1, s).start()

            pl.when(spot == 0)(begin)
            if s > 0:
                pl.when((spot > 0) & (spot <= s))(go_on)

    def combine(g, kind):
        rows = pl.ds(0, shard_rows[kind])
        mine = shard_at(kind, place.spot)
        for direction in range(2):

            def add(direction=direction):
                rs_copy(g, kind, direction, last - 1, last - 1).wait_recv()
                own[g, mine] += partial[g, kind, direction, last - 1, rows].astype(F32)

            pl.when(spots[direction] > 0)(add)

    def finished(g, kind, shard):
        rows = shard_at(kind, shard)
        hand_out(g, rows)
        if kind == 0:
            back_copy(g, rows).start()

    def ag_stage(g, kind, s):
        for direction in range(2):
            spot = spots[direction]
            shard = shard_of(direction, spot - s)

            def send(direction=direction, shard=shard):
                ag_copy(g, kind, direction, shard, s).start()

            def receive(direction=direction, shard=shard, send=send, spot=spot):
                ag_copy(g, kind, direction, shard, s - 1).wait_recv()
                if s < last:
                    pl.when(spot < last)(send)
                finished(g, kind, shard)

            if s == 0:
                pl.when(spot < last)(send)
            else:
                pl.when(spot >= s)(receive)
        if s == 0:
            finished(g, kind, place.spot)

    def across_first(g):
        core_copy(g, 0).wait_recv()
        theirs = side_at(1 - place.side)
        ours = side_at(place.side)
        across_out[g] = (own[g, theirs] + core_in[g, theirs].astype(F32)).astype(BF16)
        across_copy(g).start()
        own[g, ours] += core_in[g, ours].astype(F32)

    def across_done(g):
        across_copy(g).wait_recv()
        ours = side_at(place.side)
        own[g, ours] += across_in[g].astype(F32)
        rs_stage(g, 0, 0)

    def line_first(g):
        core_copy(g, 1).wait_recv()
        rows = pl.ds(short_at, half_rows - short_at)
        own[g, rows] += core_in[g, rows].astype(F32)
        rs_stage(g, 1, 0)

    def combine_across(g):
        combine(g, 0)
        mine = shard_at(0, place.spot)
        result[g, mine] = own[g, mine].astype(BF16)
        ag_stage(g, 0, 0)

    def combine_line(g):
        combine(g, 1)
        short_out[g] = own[g, shard_at(1, place.spot)].astype(BF16)
        short_copy(g).start()

    def short_done(g):
        short_copy(g).wait_recv()
        total = short_out[g].astype(F32) + short_in[g].astype(F32)
        result[g, shard_at(1, place.spot)] = total.astype(BF16)
        ag_stage(g, 1, 0)

    def back_done(g):
        rows = side_at(1 - place.side)
        back_copy(g, rows).wait_recv()
        hand_out(g, rows)

    chains = []
    for g in range(groups):
        middle_steps = [functools.partial(rs_stage, g, 0, s) for s in range(1, last)]
        later_steps = [functools.partial(ag_stage, g, 0, s) for s in range(1, line)]
        chains.append(
            [functools.partial(across_first, g), functools.partial(across_done, g)]
            + middle_steps
            + [functools.partial(combine_across, g)]
            + later_steps
            + [functools.partial(back_done, g)]
        )
        middle_steps = [functools.partial(rs_stage, g, 1, s) for s in range(1, last)]
        later_steps = [functools.partial(ag_stage, g, 1, s) for s in range(1, line)]
        chains.append(
            [functools.partial(line_first, g)]
            + middle_steps
            + [functools.partial(combine_line, g), functools.partial(short_done, g)]
            + later_steps
        )

    def advance(chain):
        if chain:
            chain.pop(0)()

    def small_copy(k):
        return remote(
            small_buf.at[0, k],
            small_buf.at[1, k],
            small_sem.at[0, k],
            small_sem.at[1, k],
            doubling[k],
        )

    def small_round(k):
        if k == 0:
            here = small.shape[1]
            small_buf[0, 0, 0:1, 0:here] = jnp.sum(small[...], axis=0, keepdims=True)
            small_buf[0, 0, 0:1, here:] = sums[0:1, :]
            small_copy(0).start()
            return
        small_copy(k - 1).wait()
        total = small_buf[0, k - 1] + small_buf[1, k - 1]
        if k < rounds:
            small_buf[0, k] = total
            small_copy(k).start()
        else:
            small_out[...] = total

    ones = turned.shape[1] - width
    for slot in range(2):
        turned[slot, width:] = jnp.ones((ones, turned.shape[2]), BF16)
    def tiles():
        load(0)
        for g in range(groups):
            if g + 1 < groups:
                load(g + 1)
            narrow_copy(g).wait()
            turned[g % 2, :width] = narrow[g % 2].T
            for half in (away, core):
                for t in range(2):
                    wide_copy(g, half, t).wait()
                    left = turned[(g if g < 3 or t == 1 else 2) % 2]
                    tile = dot(left, wide[g % 2, t, half])
                    if g in (1, 2) or (g == 3 and t == 0):
                        spot = half * width if g == 3 else (half * 2 + t) * width
                        spot = pl.multiple_of(sum_at[g] + spot, width)
                        sums[:, pl.ds(spot, width)] = tile[width : width + LANES]
                    tile = tile[:width]
                    if g == 0 or (g == 3 and t == 1):
                        tile = tile.T
                    rows = pl.ds(t * width, width)
                    if half is away:
                        leave[g, rows, :] = tile.astype(BF16)
                    else:
                        own[g, rows, :] = tile
                if half is away:
                    if g == 0:
                        pl.semaphore_wait(barrier, greeted)
                    for kind in range(2):
                        core_copy(g, kind).start()
                yield

    work = tiles()
    halves = 2 * groups
    small_at = 0
    for at, item in enumerate(sum_order(groups, [len(chain) for chain in chains])):
        if item < 0:
            next(work, None)
            halves -= 1
        else:
            advance(chains[item])
        if halves == 0 and at % 4 == 0 and small_at <= rounds:
            small_round(small_at)
            small_at += 1
    while small_at <= rounds:
        small_round(small_at)
        small_at += 1

    for g in range(groups):
        for kind in range(2):
            core_copy(g, kind).wait_send()
            for direction in range(2):

                def sent(kind=kind, direction=direction):
                    rows = side_at(0) if kind == 0 else pl.ds(short_at, half_rows - short_at)
                    remote(
                        result.at[g, rows],
                        result.at[g, rows],
                        line_send.at[g, kind, direction],
                        ag_recv.at[g, kind, direction, 0],
                        pair,
                    ).wait_send()

                pl.when(spots[direction] < last)(sent)
        across_copy(g).wait_send()
        short_copy(g).wait_send()
        back_copy(g, side_at(place.side)).wait_send()
        rows = pl.ds(0, half_rows)
        keep_copy(g, rows).wait()
        pair_copy(g, rows, away).wait_send()
        pair_copy(g, rows, away).wait_recv()


def unpack_kernel(
    perm_t,
    low_i,
    grad_i,
    down_i,
    up_i,
    gate_i,
    cand_i,
    out_i,
    block_out,
    grad_in,
    w_gate,
    w_cand,
    w_out,
    w_up,
    w_down,
):
    for source, target in (
        (down_i, w_down),
        (up_i, w_up),
        (gate_i, w_gate),
        (cand_i, w_cand),
        (out_i, w_out),
    ):
        target[0] = source[0].astype(F32)
    block_out[...] = dot(perm_t[...], low_i[0]).astype(BF16).reshape(block_out.shape)
    grad = grad_i[0]
    high = grad.astype(BF16)
    rest = jnp.where(lax.axis_index("section") == 0, grad - high.astype(F32), 0.0)
    grad_in[...] = (dot(perm_t[...], high) + dot(perm_t[...], rest.astype(BF16))).reshape(
        grad_in.shape
    )


def unpack(packed, low, grad, perm_t, rows, width, hidden, ff):
    packed = packed.reshape(4, ff, width)
    parts, chunk = low.shape[0], low.shape[1]
    chunks = parts // rows
    seq = chunks * chunk
    tall = ff // parts
    short = tall // 2
    spread = width // tall
    per_tile = width // short

    def column_block(t):
        return (0, t % spread, t // spread)

    return pl.pallas_call(
        unpack_kernel,
        grid=(parts,),
        out_shape=[
            jax.ShapeDtypeStruct((1, rows, seq, width), BF16),
            jax.ShapeDtypeStruct((1, rows, seq, width), F32),
            jax.ShapeDtypeStruct((1, width, 2 * hidden), F32),
            jax.ShapeDtypeStruct((1, width, hidden), F32),
            jax.ShapeDtypeStruct((1, hidden, width), F32),
            jax.ShapeDtypeStruct((1, width, ff), F32),
            jax.ShapeDtypeStruct((1, ff, width), F32),
        ],
        in_specs=[
            whole(perm_t),
            pl.BlockSpec((1, chunk, width), lambda t: (t, 0, 0)),
            pl.BlockSpec((1, chunk, width), lambda t: (t, 0, 0)),
            pl.BlockSpec((1, tall, width), lambda t: (0, t, 0)),
            pl.BlockSpec((1, tall, width), lambda t: (1, t, 0)),
            pl.BlockSpec((1, tall, width), lambda t: (2, t, 0)),
            pl.BlockSpec(
                (1, short, width),
                lambda t: (3, t // per_tile * 2 * per_tile + t % per_tile, 0),
            ),
            pl.BlockSpec(
                (1, short, width),
                lambda t: (3, t // per_tile * 2 * per_tile + per_tile + t % per_tile, 0),
            ),
        ],
        out_specs=[
            pl.BlockSpec((1, 1, chunk, width), lambda t: (0, t // chunks, t % chunks, 0)),
            pl.BlockSpec((1, 1, chunk, width), lambda t: (0, t // chunks, t % chunks, 0)),
            pl.BlockSpec((1, tall, width), column_block),
            pl.BlockSpec((1, short, width), lambda t: (0, t % per_tile, t // per_tile)),
            pl.BlockSpec((1, short, width), lambda t: (0, t, 0)),
            pl.BlockSpec((1, tall, width), column_block),
            pl.BlockSpec((1, tall, width), lambda t: (0, t, 0)),
        ],
        compiler_params=pltpu.CompilerParams(vmem_limit_bytes=VMEM_LIMIT),
        name="unpack",
    )(perm_t, low, grad, packed, packed, packed, packed, packed)


def sum_gradients(operands, small, hidden, ff):
    place = Place()
    line = place.line
    rounds = len(place.doubling())
    operands = [a.reshape(-1, a.shape[-1]) for a in operands]
    tokens, width = operands[2].shape
    total = small.shape[1] + ff + 3 * hidden
    groups = 4
    half_rows = ff // 2
    side_rows = half_rows * 3 // 8
    shard = side_rows // line
    short = (half_rows - 2 * side_rows) // line
    anywhere = pl.BlockSpec(memory_space=pl.ANY)
    here = pl.BlockSpec(memory_space=pltpu.VMEM)
    packed, small_sum = pl.pallas_call(
        functools.partial(sum_kernel, line, rounds),
        out_shape=[
            jax.ShapeDtypeStruct((groups, 2, half_rows, width), BF16),
            jax.ShapeDtypeStruct((1, total), F32),
        ],
        in_specs=[anywhere] * 7 + [here],
        out_specs=[anywhere, here],
        scratch_shapes=[
            pltpu.VMEM((2, 2, 2, tokens, width), BF16),
            pltpu.VMEM((2, tokens, width), BF16),
            pltpu.VMEM((2, width + 2 * LANES, tokens), BF16),
            pltpu.VMEM((groups, half_rows, width), F32),
            pltpu.VMEM((groups, half_rows, width), BF16),
            pltpu.VMEM((groups, half_rows, width), BF16),
            pltpu.VMEM((groups, side_rows, width), BF16),
            pltpu.VMEM((groups, side_rows, width), BF16),
            pltpu.VMEM((groups, short, width), BF16),
            pltpu.VMEM((groups, short, width), BF16),
            pltpu.VMEM((groups, 2, 2, line - 1, max(shard, short), width), BF16),
            pltpu.VMEM((groups, half_rows, width), BF16),
            pltpu.VMEM((2, rounds, 1, total), F32),
            pltpu.VMEM((LANES, ff + 3 * hidden), F32),
            pltpu.SemaphoreType.DMA((2, 2, 2)),
            pltpu.SemaphoreType.DMA((2,)),
            pltpu.SemaphoreType.DMA((2, groups, 2)),
            pltpu.SemaphoreType.DMA((2, groups)),
            pltpu.SemaphoreType.DMA((2, groups)),
            pltpu.SemaphoreType.DMA((2, groups)),
            pltpu.SemaphoreType.DMA((groups, 2, 2)),
            pltpu.SemaphoreType.DMA((groups, 2, 2, line - 1)),
            pltpu.SemaphoreType.DMA((groups, 2, 2, line - 1)),
            pltpu.SemaphoreType.DMA((groups,)),
            pltpu.SemaphoreType.DMA((2, groups)),
            pltpu.SemaphoreType.DMA((2, rounds)),
        ],
        compiler_params=pltpu.CompilerParams(
            collective_id=2, has_side_effects=True, vmem_limit_bytes=VMEM_LIMIT
        ),
        name="sum_gradients",
    )(*operands, small)
    dp_size = lax.axis_size("dp")
    inner = 2 * line
    if dp_size > inner:
        members = [list(range(i, dp_size, inner)) for i in range(inner)]
        packed, small_sum = lax.psum((packed, small_sum), "dp", axis_index_groups=members)
    return packed, small_sum


def split_small(small, width, hidden, ff):
    sizes = (width, width, width, width, ff, 2 * hidden, hidden)
    out = []
    at = 0
    for n in sizes:
        out.append(small[:, at : at + n])
        at += n
    return out


def body(tokens, resets, cotangent, *stacked):
    rows, _, width = tokens.shape
    hidden = stacked[3].shape[2]
    ff = stacked[8].shape[2]
    low, grad_in, perm_t, (*operands, small) = local_grads(tokens, resets, cotangent, stacked)
    packed, small_sum = sum_gradients(operands, small, hidden, ff)
    block_out, grad_in, w_gate, w_cand, w_out, w_up, w_down = unpack(
        packed, low, grad_in, perm_t, rows, width, hidden, ff
    )
    g_one, b_out, g_two, b_down, b_up, b_gate, b_cand = split_small(small_sum, width, hidden, ff)
    grads = (g_one, w_gate, b_gate, w_cand, b_cand, w_out, b_out, g_two, w_up, b_up, w_down, b_down)
    return (block_out, grad_in) + grads


def solution(mesh):
    vector = P("section", None)
    matrix = P("section", None, None)
    weight_specs = (
        vector,
        matrix,
        vector,
        matrix,
        vector,
        matrix,
        vector,
        vector,
        matrix,
        vector,
        matrix,
        vector,
    )
    tokens = P(("dp", "rep"), None, None)
    by_rows = P("section", ("dp", "rep"), None, None)
    return jax.shard_map(
        body,
        mesh=mesh,
        in_specs=(tokens, P(("dp", "rep"), None), tokens) + weight_specs,
        out_specs=(by_rows, by_rows) + weight_specs,
        check_vma=False,
    )
```

time: 374 us -> 242 us (0.65)
  waiting for transfers between devices: 106 us -> 0 us
  Pallas kernels: 136 us -> 233 us
  blocking collectives: 63.4 us -> 0 us
  matrix products: 29.9 us -> 0 us
  between operations: 14.2 us -> 0.87 us
  other arithmetic: 14.3 us -> 1.66 us
  local copies, waits for them, and re-layouts: 10 us -> 5.47 us
    psum x1 -> x0, waiting for transfers between devices: 106 us -> none  [body(): lax.psum(tuple((g.astype(BF16) for g in large)) + (small,), ('dp', 'rep'))]
    pallas_call x2 -> x3, Pallas kernels: 136 us -> 233 us  [the longest x1 118 us: run_blocks(): pl.pallas_call(functools.partial(blocks_kernel, rows, chunks), grid=(2 *...]
    psum x1 -> x0, blocking collectives: 63.4 us -> none  [body(): lax.psum(tuple((g.astype(BF16) for g in large)) + (small,), ('dp', 'rep'))]
    dot_general x5 -> x0, matrix products: 29.9 us -> none  [weight_grad(): lax.dot_general(a, b, (((0,), (0,)), ((), ())), preferred_element_type=F32)]
    broadcast_in_dim x5 -> x0, other arithmetic: 12.5 us -> none  [body(): return (block_out, grad_in) + tuple((g[None] for g in grads))]
    unnamed x34 -> x0, local copies, waits for them, and re-layouts: 6.66 us -> none
  transfers between devices with their start and end apart: 1 -> 0, of which waited for: 1 -> 0; matrix products, arithmetic and copies ran while one was open for 0% -> 0% of each run, Pallas kernels for 0% -> 0%
where the time goes in v3:
time: 242 us; the launch traced here: 241 us
  Pallas kernels  233 us (96%)
  local copies, waits for them, and re-layouts  5.47 us (2%)
    pallas_call x1, Pallas kernels, run_blocks(): pl.pallas_call(functools.partial(blocks_kernel, rows, chunks), grid=(2 *...  118 us
    pallas_call x1, Pallas kernels, sum_gradients(): pl.pallas_call(functools.partial(sum_kernel, line, rounds), out_shape=[ja...  100 us
    pallas_call x1, Pallas kernels, unpack(): pl.pallas_call(unpack_kernel, grid=(parts,), out_shape=[jax.ShapeDtypeStr...  14.8 us

profile of v3, /device:TPU:0, one launch (start us, length us, event | category | flops | bytes accessed | tf_op | source)
XLA Modules:
  0.0 241.4 jit_solution(8906956563696734862)
XLA Ops:
  0.7 0.7 subtract_convert_fusion
  1.4 0.1 reshape.57
  1.5 0.1 copy.30
  1.6 0.1 broadcast_in_dim.7
  1.7 0.9 fusion.1
  2.6 1.3 broadcast_in_dim.8.keep
  3.9 118.3 %blocks.1 = (bf16[8,256,2048]{2,1,0:T(8,128)(2,1)}, bf16[8,256,2048]{2,1,0:T(8,128)(2,1)}, bf16[8,256,512]{2,1,0:T(8,128)(2,1)}, bf16[8,256,512]{2,1,0:T(8,128)(...) custom-call(bf16[2,1024,512]{2,1,0:T(8,128)(2,1)} %tok.1, ...), custom_call_target="tpu_custom_call" | custom-call | tf_op jit(solution)/shard_map/blocks/pallas_call | solution.py:454
  122.3 100.2 %sum_gradients.1 = (bf16[4,2,1024,512]{3,2,1,0:T(8,128)(2,1)}, f32[1,7168]{1,0:T(1,128)}) custom-call(bf16[2048,2048]{1,0:T(8,128)(2,1)} %bitcast.19, bf16[2048,2048]{1,0:T(8,128)(2,1)} %bitcast.20, bf16[2048,512]{1,0:T(8,128)(2,1)} %bitcast.24, bf16[2048,2048]{1,0:T(8,128)(2,1)} %bitcast.21, bf16[2048,512]{1,0:T(8,128)(2,1)} %bitcast.25, ...), custom_call_target="tpu_custom_call" | custom-call | tf_op jit(solution)/shard_map/sum_gradients/pallas_call | solution.py:1077
  222.5 1.3 slice.23
  223.8 1.3 fusion.4
  225.0 1.3 fusion.5
  226.4 14.8 %unpack.1 = (bf16[1,2,1024,512]{3,2,1,0:T(8,128)(2,1)}, f32[1,2,1024,512]{3,2,1,0:T(8,128)}, f32[1,512,2048]{2,1,0:T(8,128)}, f32[1,512,1024]{2,1,0:T(8,128)}, f...) custom-call(bf16[256,256]{1,0:T(8,128)(2,1)} %get-tuple-element.59.perm_t, ...), custom_call_target="tpu_custom_call" | custom-call | tf_op jit(solution)/shard_map/unpack/pallas_call | solution.py:1021
  (3 shorter events, 0.0 us)

commit v4 on v3

--- a/solution.py
+++ b/solution.py
@@ -3,6 +3,7 @@
 
 import jax
 import jax.numpy as jnp
+import numpy as np
 from jax import lax
 from jax.experimental import pallas as pl
 from jax.experimental.pallas import tpu as pltpu
@@ -76,40 +77,52 @@
         self.row = jnp.where(first, phase % rows, phase // 2)
         base = self.row * chunks
         last = chunks - 1
-        before = jnp.where(first, last, jnp.maximum(base - chunks, jnp.where(self.row == 0, last, 0)))
-        after = jnp.where(first, rows * chunks - 1, base + last)
-        self.mixer = jnp.where(self.forward, base + jnp.minimum(self.at, last), after)
-        self.feed = jnp.where(self.forward, base + jnp.maximum(self.at - 1, 0), after)
-        self.back_feed = jnp.where(self.forward, before, base + jnp.maximum(last - self.at, 0))
-        self.back_mixer = jnp.where(self.forward, before, base + jnp.minimum(chunks - self.at, last))
-        self.next_mixer = jnp.minimum(self.mixer + 1, rows * chunks - 1)
-        later = jnp.minimum(base + self.at + 1, rows * chunks - 1)
-        later = jnp.where(self.forward, base, jnp.minimum(later, base + chunks))
-        later = jnp.minimum(later, rows * chunks - 1)
+        self.mixer = base + jnp.minimum(self.at, last)
+        self.feed = base + jnp.maximum(self.at - 1, 0)
+        self.back_feed = base + jnp.maximum(last - self.at, 0)
+        self.back_mixer = base + jnp.minimum(chunks - self.at, last)
+        total = rows * chunks
+        self.next_mixer = jnp.minimum(self.mixer + 1, total - 1)
+        later = jnp.minimum(base + self.at + 1, total - 1)
         self.next_back = later // chunks * chunks + last - later % chunks
 
 
 def blocks_kernel(
     rows,
     chunks,
-    first_tok,
     tok,
-    first_cot,
     cot,
-    keep,
+    w_gate_all,
+    w_cand_all,
+    w_out_all,
+    w_up_all,
+    w_down_all,
+    keep_rows,
     perm,
     g_one,
-    w_gate,
     b_gate,
-    w_cand,
     b_cand,
-    w_out,
     b_out,
     g_two,
+    b_up,
+    b_down,
+    operands_all,
+    active_all,
+    low_all,
+    down_all,
+    up_all,
+    mix_all,
+    gate_all,
+    cand_all,
+    grad_all,
+    small_o,
+    raw,
+    keep,
+    w_gate,
+    w_cand,
+    w_out,
     w_up,
-    b_up,
     w_down,
-    b_down,
     operands_o,
     active_o,
     low_o,
@@ -118,8 +131,7 @@
     mix_o,
     gate_o,
     cand_o,
-    grad_in,
-    small_o,
+    grad_o,
     ratio_s,
     slopes_s,
     middle_s,
@@ -134,21 +146,56 @@
     normed_two_s,
     grad_middle_s,
     mix_s,
+    load_sem,
+    stage_sem,
     send_sem,
     input_sem,
     back_send_sem,
     received_sem,
 ):
-    c = pl.program_id(0)
     section = lax.axis_index("section")
     partner = 1 - section
-    step = Step(c, rows, chunks)
-    _, tokens, width = tok.shape
+    chunk, width = coming.shape
     hidden = w_cand.shape[1]
     ff = w_up.shape[1]
-    span = tokens // LANES
+    span = chunk // LANES
     total = rows * chunks
-    final = 2 * rows * (chunks + 1) - 1
+    steps = 2 * rows * (chunks + 1)
+    stages = (
+        (operands_o, operands_all),
+        (active_o, active_all),
+        (low_o, low_all),
+        (down_o, down_all),
+        (up_o, up_all),
+        (mix_o, mix_all),
+        (gate_o, gate_all),
+        (cand_o, cand_all),
+        (grad_o, grad_all),
+    )
+
+    def stage_copy(which, at_chunk):
+        source, target = stages[which]
+        slot = at_chunk % 2
+        return pltpu.make_async_copy(
+            source.at[slot], target.at[at_chunk], stage_sem.at[which, slot]
+        )
+
+    def load_copy(which):
+        pairs = (
+            (w_gate_all, w_gate),
+            (w_cand_all, w_cand),
+            (w_out_all, w_out),
+            (w_up_all, w_up),
+            (w_down_all, w_down),
+        )
+        return pltpu.make_async_copy(*pairs[which], load_sem.at[which])
+
+    def raw_copy(source):
+        return pltpu.make_async_copy(source, raw, load_sem.at[5])
+
+    def raw_chunk(at_chunk):
+        start = pl.multiple_of(at_chunk % chunks * chunk, chunk)
+        return raw[at_chunk // chunks, pl.ds(start, chunk)]
 
     def chunk_copy(slot):
         return remote(
@@ -172,233 +219,300 @@
         part = jnp.sum(values.reshape(-1, LANES, width), axis=0)
         small_o[:, which * width : (which + 1) * width] += part
 
-    @pl.when(c == 0)
-    def _():
-        partner_barrier_signal(partner)
-        small_o[...] = jnp.zeros_like(small_o)
-        coming[...] = dot(perm[...], first_tok[0]).astype(BF16)
-        coming_back[...] = dot(perm[...], first_cot[0]).astype(BF16)
-        pl.semaphore_wait(pltpu.get_barrier_semaphore(), 1)
-
-    @pl.when(step.forward & (step.at == 0))
-    def _():
-        carry[...] = jnp.zeros_like(carry)
-
-    @pl.when(jnp.logical_not(step.forward) & (step.at == 0))
-    def _():
-        carry_back[...] = jnp.zeros_like(carry_back)
-
-    @pl.when(step.forward & (step.at < chunks) & (section == 0))
-    def _():
-        inputs[step.mixer] = coming[...]
-
-    @pl.when(step.forward & (step.at < chunks) & (section == 1))
-    def _():
-        chunk_copy(step.mixer).wait_recv()
-
-    @pl.when(jnp.logical_not(step.forward) & (step.at < chunks) & (section == 0))
-    def _():
-        back_copy(step.back_feed).wait_recv()
-        coming_back[...] = received[step.back_feed]
-
-    def mixer():
-        at_chunk = step.mixer
-        x = inputs[at_chunk].astype(F32)
-        normed = (x * inv_scale(x) * g_one[...]).astype(BF16)
-        operands_o[0, :, :width] = normed
-        yield
-        for at in range(0, hidden, WIDTH):
-            cols = slice(at, at + WIDTH)
-            cols_in = slice(hidden + at, hidden + at + WIDTH)
-            pre_f = dot(normed, w_gate[:, cols])
-            pre_i = dot(normed, w_gate[:, cols_in])
-            cand = dot(normed, w_cand[:, cols]) + b_cand[:, cols]
-            u = jnp.exp(jnp.minimum((-LN4 - b_gate[:, cols]) - pre_f, EXP_TOP))
-            v = jnp.exp(jnp.minimum((-LN4 - b_gate[:, cols_in]) - pre_i, EXP_TOP))
-            d = 1.0 / (0.5 + u + v)
-            ratio_f = (0.25 + v) * d
-            ratio_i = (0.25 + u) * d
-            ratio_s[at_chunk, :, cols] = ratio_f
-            keep_w = jnp.concatenate([keep[0]] * (WIDTH // 128), axis=1)
-            decay = ratio_f * keep_w
-            drive = ratio_i * cand
-            product = decay[0:LANES]
-            accum = drive[0:LANES]
-            for j in range(1, span):
-                r = slice(j * LANES, (j + 1) * LANES)
-                accum = decay[r] * accum + drive[r]
-                product = decay[r] * product
-            state, carry[:, cols] = scan_segments(product, accum, carry[:, cols], False)
-            before = []
-            after = []
-            for j in range(span):
-                r = slice(j * LANES, (j + 1) * LANES)
-                before.append(state)
-                state = decay[r] * state + drive[r]
-                after.append(state)
-            operands_o[0, :, width + at : width + at + WIDTH] = jnp.concatenate(
-                after, axis=0
-            ).astype(BF16)
-            lever = keep_w * jnp.concatenate(before, axis=0) - cand
-            slopes_s[at_chunk, :, cols] = (lever * ((u * d) * ratio_f)).astype(BF16)
-            slopes_s[at_chunk, :, cols_in] = (-lever * ((v * d) * ratio_i)).astype(BF16)
+    def blocks_step(c):
+        step = Step(c, rows, chunks)
+
+        @pl.when(c == 1)
+        def _():
+            load_copy(3).wait()
+            load_copy(4).wait()
+
+        @pl.when(step.forward & (step.at == 0))
+        def _():
+            carry[...] = jnp.zeros_like(carry)
+
+        @pl.when(jnp.logical_not(step.forward) & (step.at == 0))
+        def _():
+            carry_back[...] = jnp.zeros_like(carry_back)
+
+        @pl.when(step.forward & (step.at < chunks) & (section == 0))
+        def _():
+            inputs[step.mixer] = coming[...]
+
+        @pl.when(step.forward & (step.at < chunks) & (section == 1))
+        def _():
+            chunk_copy(step.mixer).wait_recv()
+
+        @pl.when(jnp.logical_not(step.forward) & (step.at < chunks) & (section == 0))
+        def _():
+            back_copy(step.back_feed).wait_recv()
+            coming_back[...] = received[step.back_feed]
+
+        @pl.when(step.forward & (step.at < chunks) & (step.mixer >= 2))
+        def _():
+            stage_copy(0, step.mixer).wait()
+
+        @pl.when(step.forward & (step.at > 0) & (step.feed >= 2))
+        def _():
+            for which in (1, 2):
+                stage_copy(which, step.feed).wait()
+
+        @pl.when(jnp.logical_not(step.forward) & (step.at < chunks) & (step.row * chunks + step.at >= 2))
+        def _():
+            for which in (3, 4, 5):
+                stage_copy(which, step.back_feed).wait()
+
+        @pl.when(jnp.logical_not(step.forward) & (step.at > 0) & (step.row * chunks + step.at >= 3))
+        def _():
+            for which in (6, 7, 8):
+                stage_copy(which, step.back_mixer).wait()
+
+        def mixer():
+            at_chunk = step.mixer
+            slot = at_chunk % 2
+            x = inputs[at_chunk].astype(F32)
+            normed = (x * inv_scale(x) * g_one[...]).astype(BF16)
+            operands_o[slot, :, :width] = normed
             yield
-        mixed = dot(operands_o[0, :, width : width + hidden], w_out[...])
-        yield
-        middle = x + (mixed + b_out[...])
-        normed_two = (middle * inv_scale(middle) * g_two[...]).astype(BF16)
-        operands_o[0, :, width + hidden :] = normed_two
-        yield
-        middle_s[at_chunk] = middle
-        normed_two_s[...] = normed_two
-
-    def feed():
-        at_chunk = step.feed
-        for at in range(0, ff, WIDTH):
-            cols = slice(at, at + WIDTH)
-            up = dot(normed_two_s[...], w_up[:, cols]) + b_up[:, cols]
-            square = up * up
-            half = 0.5 + 0.5 * jnp.tanh(up * (GELU_A + (GELU_A * GELU_B) * square))
-            act = up * half
-            active_o[0, :, cols] = act.astype(BF16)
-            slope = half + act * (1.0 - half) * (2 * GELU_A + (6 * GELU_A * GELU_B) * square)
-            slope_up_s[at_chunk, :, cols] = slope.astype(BF16)
-            if at % (2 * WIDTH):
+            for at in range(0, hidden, WIDTH):
+                cols = slice(at, at + WIDTH)
+                cols_in = slice(hidden + at, hidden + at + WIDTH)
+                pre_f = dot(normed, w_gate[:, cols])
+                pre_i = dot(normed, w_gate[:, cols_in])
+                cand = dot(normed, w_cand[:, cols]) + b_cand[:, cols]
+                u = jnp.exp(jnp.minimum((-LN4 - b_gate[:, cols]) - pre_f, EXP_TOP))
+                v = jnp.exp(jnp.minimum((-LN4 - b_gate[:, cols_in]) - pre_i, EXP_TOP))
+                d = 1.0 / (0.5 + u + v)
+                ratio_f = (0.25 + v) * d
+                ratio_i = (0.25 + u) * d
+                ratio_s[at_chunk, :, cols] = ratio_f
+                keep_w = jnp.concatenate([keep[at_chunk]] * (WIDTH // 128), axis=1)
+                decay = ratio_f * keep_w
+                drive = ratio_i * cand
+                product = decay[0:LANES]
+                accum = drive[0:LANES]
+                for j in range(1, span):
+                    r = slice(j * LANES, (j + 1) * LANES)
+                    accum = decay[r] * accum + drive[r]
+                    product = decay[r] * product
+                state, carry[:, cols] = scan_segments(product, accum, carry[:, cols], False)
+                before = []
+                after = []
+                for j in range(span):
+                    r = slice(j * LANES, (j + 1) * LANES)
+                    before.append(state)
+                    state = decay[r] * state + drive[r]
+                    after.append(state)
+                operands_o[slot, :, width + at : width + at + WIDTH] = jnp.concatenate(
+                    after, axis=0
+                ).astype(BF16)
+                lever = keep_w * jnp.concatenate(before, axis=0) - cand
+                slopes_s[at_chunk, :, cols] = (lever * ((u * d) * ratio_f)).astype(BF16)
+                slopes_s[at_chunk, :, cols_in] = (-lever * ((v * d) * ratio_i)).astype(BF16)
                 yield
-        down = dot(active_o[0], w_down[...])
-        yield
-        low_o[0] = (middle_s[at_chunk] + (down + b_down[...])).astype(BF16)
-
-    def reorder():
-        yield
-        yield
-        coming[...] = dot(perm[...], tok[0]).astype(BF16)
-
-    def back_feed():
-        at_chunk = step.back_feed
-        grad_down = coming_back[...]
-        down_o[0] = grad_down
-        yield
-        for at in range(0, ff, WIDTH):
-            cols = slice(at, at + WIDTH)
-            grad_active = dot_nt(grad_down, w_down[cols, :])
-            slope = slope_up_s[at_chunk, :, cols].astype(F32)
-            up_o[0, :, cols] = (grad_active * slope).astype(BF16)
-            if at % (2 * WIDTH):
+            mixed = dot(operands_o[slot, :, width : width + hidden], w_out[...])
+            yield
+            middle = x + (mixed + b_out[...])
+            normed_two = (middle * inv_scale(middle) * g_two[...]).astype(BF16)
+            operands_o[slot, :, width + hidden :] = normed_two
+            yield
+            middle_s[at_chunk] = middle
+            normed_two_s[...] = normed_two
+
+        def feed():
+            at_chunk = step.feed
+            slot = at_chunk % 2
+            for at in range(0, ff, WIDTH):
+                cols = slice(at, at + WIDTH)
+                up = dot(normed_two_s[...], w_up[:, cols]) + b_up[:, cols]
+                square = up * up
+                half = 0.5 + 0.5 * jnp.tanh(up * (GELU_A + (GELU_A * GELU_B) * square))
+                act = up * half
+                active_o[slot, :, cols] = act.astype(BF16)
+                slope = half + act * (1.0 - half) * (2 * GELU_A + (6 * GELU_A * GELU_B) * square)
+                slope_up_s[at_chunk, :, cols] = slope.astype(BF16)
+                if at % (2 * WIDTH):
+                    yield
+            down = dot(active_o[slot], w_down[...])
+            yield
+            low_o[slot] = (middle_s[at_chunk] + (down + b_down[...])).astype(BF16)
+
+        def reorder():
+            yield
+            yield
+            coming[...] = dot(perm[...], raw_chunk(step.next_mixer)).astype(BF16)
+
+        def back_feed():
+            at_chunk = step.back_feed
+            slot = at_chunk % 2
+            grad_down = coming_back[...]
+            down_o[slot] = grad_down
+            yield
+            for at in range(0, ff, WIDTH):
+                cols = slice(at, at + WIDTH)
+                grad_active = dot_nt(grad_down, w_down[cols, :])
+                slope = slope_up_s[at_chunk, :, cols].astype(F32)
+                up_o[slot, :, cols] = (grad_active * slope).astype(BF16)
+                if at % (2 * WIDTH):
+                    yield
+            q = dot_nt(up_o[slot], w_up[...])
+            yield
+            dy = grad_down.astype(F32)
+            add_small(3, dy)
+            middle = middle_s[at_chunk]
+            r = inv_scale(middle)
+            scaled = middle * r
+            add_small(2, q * scaled)
+            weighted = q * g_two[...]
+            grad_middle = dy + r * (
+                weighted - scaled * jnp.mean(weighted * scaled, axis=-1, keepdims=True)
+            )
+            add_small(1, grad_middle)
+            grad_mix = grad_middle.astype(BF16)
+            mix_o[slot] = grad_mix
+            yield
+            yield
+            grad_middle_s[...] = grad_middle
+            mix_s[...] = grad_mix
+
+        def back_mixer():
+            at_chunk = step.back_mixer
+            slot = at_chunk % 2
+            for at in range(0, hidden, WIDTH):
+                cols = slice(at, at + WIDTH)
+                cols_in = slice(hidden + at, hidden + at + WIDTH)
+                grad_state = dot_nt(mix_s[...], w_out[cols, :])
+                ratio_f = ratio_s[at_chunk, :, cols]
+                decay = ratio_f * jnp.concatenate([keep[at_chunk]] * (WIDTH // 128), axis=1)
+                last = slice((span - 1) * LANES, span * LANES)
+                product = decay[last]
+                accum = decay[last] * grad_state[last]
+                for j in range(span - 2, -1, -1):
+                    rj = slice(j * LANES, (j + 1) * LANES)
+                    accum = decay[rj] * (grad_state[rj] + accum)
+                    product = decay[rj] * product
+                later, carry_back[:, cols] = scan_segments(product, accum, carry_back[:, cols], True)
+                parts = [None] * span
+                for j in range(span - 1, -1, -1):
+                    rj = slice(j * LANES, (j + 1) * LANES)
+                    carried = grad_state[rj] + later
+                    parts[j] = carried
+                    later = decay[rj] * carried
+                carried = jnp.concatenate(parts, axis=0)
+                gate_o[slot, :, cols] = (carried * slopes_s[at_chunk, :, cols].astype(F32)).astype(BF16)
+                gate_o[slot, :, cols_in] = (
+                    carried * slopes_s[at_chunk, :, cols_in].astype(F32)
+                ).astype(BF16)
+                cand_o[slot, :, cols] = (carried * (1.0 - ratio_f)).astype(BF16)
                 yield
-        q = dot_nt(up_o[0], w_up[...])
-        yield
-        dy = grad_down.astype(F32)
-        add_small(3, dy)
-        middle = middle_s[at_chunk]
-        r = inv_scale(middle)
-        scaled = middle * r
-        add_small(2, q * scaled)
-        weighted = q * g_two[...]
-        grad_middle = dy + r * (
-            weighted - scaled * jnp.mean(weighted * scaled, axis=-1, keepdims=True)
-        )
-        add_small(1, grad_middle)
-        grad_mix = grad_middle.astype(BF16)
-        mix_o[0] = grad_mix
-        yield
-        yield
-        grad_middle_s[...] = grad_middle
-        mix_s[...] = grad_mix
-
-    def back_mixer():
-        at_chunk = step.back_mixer
-        for at in range(0, hidden, WIDTH):
-            cols = slice(at, at + WIDTH)
-            cols_in = slice(hidden + at, hidden + at + WIDTH)
-            grad_state = dot_nt(mix_s[...], w_out[cols, :])
-            ratio_f = ratio_s[at_chunk, :, cols]
-            decay = ratio_f * jnp.concatenate([keep[0]] * (WIDTH // 128), axis=1)
-            last = slice((span - 1) * LANES, span * LANES)
-            product = decay[last]
-            accum = decay[last] * grad_state[last]
-            for j in range(span - 2, -1, -1):
-                rj = slice(j * LANES, (j + 1) * LANES)
-                accum = decay[rj] * (grad_state[rj] + accum)
-                product = decay[rj] * product
-            later, carry_back[:, cols] = scan_segments(product, accum, carry_back[:, cols], True)
-            parts = [None] * span
-            for j in range(span - 1, -1, -1):
-                rj = slice(j * LANES, (j + 1) * LANES)
-                carried = grad_state[rj] + later
-                parts[j] = carried
-                later = decay[rj] * carried
-            carried = jnp.concatenate(parts, axis=0)
-            gate_o[0, :, cols] = (carried * slopes_s[at_chunk, :, cols].astype(F32)).astype(BF16)
-            gate_o[0, :, cols_in] = (
-                carried * slopes_s[at_chunk, :, cols_in].astype(F32)
-            ).astype(BF16)
-            cand_o[0, :, cols] = (carried * (1.0 - ratio_f)).astype(BF16)
+            p = dot_nt(gate_o[slot], w_gate[...]) + dot_nt(cand_o[slot], w_cand[...])
             yield
-        p = dot_nt(gate_o[0], w_gate[...]) + dot_nt(cand_o[0], w_cand[...])
-        yield
-        x = inputs[at_chunk].astype(F32)
-        r = inv_scale(x)
-        scaled = x * r
-        add_small(0, p * scaled)
-        weighted = p * g_one[...]
-        grad_in[0] = grad_middle_s[...] + r * (
-            weighted - scaled * jnp.mean(weighted * scaled, axis=-1, keepdims=True)
-        )
-
-    def back_reorder():
-        yield
-        yield
-        coming_back[...] = dot(perm[...], cot[0]).astype(BF16)
-
-    opening = step.at == 0
-    closing = step.at == chunks
-    between = jnp.logical_not(opening | closing)
-    backward = jnp.logical_not(step.forward)
-
-    @pl.when(step.forward & opening)
-    def _():
-        interleave(mixer(), reorder())
-
-    @pl.when(step.forward & between)
-    def _():
-        interleave(mixer(), feed(), reorder())
-
-    @pl.when(step.forward & closing)
-    def _():
-        interleave(feed())
-
-    @pl.when(backward & opening)
-    def _():
-        interleave(back_feed(), back_reorder())
-
-    @pl.when(backward & between)
-    def _():
-        interleave(back_feed(), back_mixer(), back_reorder())
-
-    @pl.when(backward & closing)
-    def _():
-        interleave(back_mixer())
-
-    @pl.when(step.forward & jnp.logical_not(opening) & (section == 0))
-    def _():
-        send[step.feed] = low_o[0]
-        chunk_copy(step.feed).start()
-
-    @pl.when(backward & jnp.logical_not(opening) & (section == 1))
-    def _():
-        send[step.back_mixer] = grad_in[0].astype(BF16)
-        back_copy(step.back_mixer).start()
-
-    @pl.when((c == final) & (section == 0))
+            x = inputs[at_chunk].astype(F32)
+            r = inv_scale(x)
+            scaled = x * r
+            add_small(0, p * scaled)
+            weighted = p * g_one[...]
+            grad_input = grad_middle_s[...] + r * (
+                weighted - scaled * jnp.mean(weighted * scaled, axis=-1, keepdims=True)
+            )
+            grad_o[slot] = grad_input.astype(BF16)
+
+        def back_reorder():
+            yield
+            yield
+            coming_back[...] = dot(perm[...], raw_chunk(step.next_back)).astype(BF16)
+
+        opening = step.at == 0
+        closing = step.at == chunks
+        between = jnp.logical_not(opening | closing)
+        backward = jnp.logical_not(step.forward)
+
+        @pl.when(step.forward & opening)
+        def _():
+            interleave(mixer(), reorder())
+
+        @pl.when(step.forward & between)
+        def _():
+            interleave(mixer(), feed(), reorder())
+
+        @pl.when(step.forward & closing)
+        def _():
+            interleave(feed())
+
+        @pl.when(backward & opening)
+        def _():
+            interleave(back_feed(), back_reorder())
+
+        @pl.when(backward & between)
+        def _():
+            interleave(back_feed(), back_mixer(), back_reorder())
+
+        @pl.when(backward & closing)
+        def _():
+            interleave(back_mixer())
+
+        @pl.when(step.forward & jnp.logical_not(closing))
+        def _():
+            stage_copy(0, step.mixer).start()
+
+        @pl.when(step.forward & jnp.logical_not(opening))
+        def _():
+            for which in (1, 2):
+                stage_copy(which, step.feed).start()
+
+        @pl.when(backward & jnp.logical_not(closing))
+        def _():
+            for which in (3, 4, 5):
+                stage_copy(which, step.back_feed).start()
+
+        @pl.when(backward & jnp.logical_not(opening))
+        def _():
+            for which in (6, 7, 8):
+                stage_copy(which, step.back_mixer).start()
+
+        @pl.when(step.forward & jnp.logical_not(opening) & (section == 0))
+        def _():
+            send[step.feed] = low_o[step.feed % 2]
+            chunk_copy(step.feed).start()
+
+        @pl.when(backward & jnp.logical_not(opening) & (section == 1))
+        def _():
+            send[step.back_mixer] = grad_o[step.back_mixer % 2]
+            back_copy(step.back_mixer).start()
+
+    partner_barrier_signal(partner)
+    pl.when(section == 0)(lambda: raw_copy(tok).start())
+    pl.when(section == 1)(lambda: raw_copy(cot).start())
+    for which in range(5):
+        load_copy(which).start()
+    small_o[...] = jnp.zeros_like(small_o)
+    raw_copy(tok).wait()
+    coming[...] = dot(perm[...], raw_chunk(0)).astype(BF16)
+    coming_back[...] = dot(perm[...], raw_chunk(chunks - 1)).astype(BF16)
+    pl.semaphore_wait(pltpu.get_barrier_semaphore(), 1)
+    for at_chunk in range(total):
+        row = keep_rows[at_chunk : at_chunk + 1, :]
+        keep[at_chunk] = jnp.broadcast_to(row, (128, chunk)).T
+    for which in range(3):
+        load_copy(which).wait()
+
+    @pl.loop(0, steps)
+    def _(c):
+        blocks_step(c)
+
+    @pl.when(section == 0)
     def _():
         for slot in range(total):
             chunk_copy(slot).wait_send()
 
-    @pl.when((c == final) & (section == 1))
+    @pl.when(section == 1)
     def _():
         for slot in range(total):
             back_copy(slot).wait_send()
+
+    for which in range(len(stages)):
+        for slot in range(2):
+            stage_copy(which, slot).wait()
 
 
 def whole(array):
@@ -410,62 +524,27 @@
     rows, seq, width = tokens.shape
     chunks = seq // chunk
     total = rows * chunks
-    hidden = weights[3].shape[1]
-    ff = weights[8].shape[1]
-
-    def index(name):
-        def of_step(c):
-            return (getattr(Step(c, rows, chunks), name), 0, 0)
-
-        return of_step
-
-    def rows_of(name):
-        def of_step(c):
-            at = getattr(Step(c, rows, chunks), name)
-            return (at // chunks, at % chunks, 0)
-
-        return of_step
-
-    def keep_of(c):
-        step = Step(c, rows, chunks)
-        return (jnp.where(step.forward, step.mixer, step.back_mixer), 0, 0)
-
-    def given(columns, dtype, name):
-        shape = jax.ShapeDtypeStruct((total, chunk, columns), dtype)
-        return shape, pl.BlockSpec((1, chunk, columns), index(name))
-
-    outs = [
-        given(2 * width + hidden, BF16, "mixer"),
-        given(ff, BF16, "feed"),
-        given(width, BF16, "feed"),
-        given(width, BF16, "back_feed"),
-        given(ff, BF16, "back_feed"),
-        given(width, BF16, "back_feed"),
-        given(2 * hidden, BF16, "back_mixer"),
-        given(hidden, BF16, "back_mixer"),
-        given(width, F32, "back_mixer"),
-        (
-            jax.ShapeDtypeStruct((LANES, 4 * width), F32),
-            pl.BlockSpec((LANES, 4 * width), lambda c: (0, 0)),
-        ),
-    ]
-    part = (1, chunk, width)
-    once = pl.Buffered(1)
+    g_one, w_gate, b_gate, w_cand, b_cand, w_out, b_out, g_two, w_up, b_up, w_down, b_down = weights
+    hidden = w_cand.shape[1]
+    ff = w_up.shape[1]
+    large = (w_gate, w_cand, w_out, w_up, w_down)
+    little = (keep, perm, g_one, b_gate, b_cand, b_out, g_two, b_up, b_down)
+    columns = (2 * width + hidden, ff, width, width, ff, width, 2 * hidden, hidden, width)
+    anywhere = pl.BlockSpec(memory_space=pl.ANY)
+    here = pl.BlockSpec(memory_space=pltpu.VMEM)
     return pl.pallas_call(
         functools.partial(blocks_kernel, rows, chunks),
-        grid=(2 * rows * (chunks + 1),),
-        out_shape=[o[0] for o in outs],
-        in_specs=[
-            pl.BlockSpec(part, lambda c: (0, 0, 0), pipeline_mode=once),
-            pl.BlockSpec(part, rows_of("next_mixer")),
-            pl.BlockSpec(part, lambda c: (0, chunks - 1, 0), pipeline_mode=once),
-            pl.BlockSpec(part, rows_of("next_back")),
-            pl.BlockSpec((1, chunk, 128), keep_of),
-            whole(perm),
+        out_shape=[jax.ShapeDtypeStruct((total, chunk, n), BF16) for n in columns]
+        + [jax.ShapeDtypeStruct((LANES, 4 * width), F32)],
+        in_specs=[anywhere] * 7 + [here] * len(little),
+        out_specs=[anywhere] * len(columns) + [here],
+        scratch_shapes=[
+            pltpu.VMEM(tokens.shape, BF16),
+            pltpu.VMEM((total, chunk, 128), F32),
         ]
-        + [whole(w) for w in weights],
-        out_specs=[o[1] for o in outs],
-        scratch_shapes=[
+        + [pltpu.VMEM(w.shape, BF16) for w in large]
+        + [pltpu.VMEM((2, chunk, n), BF16) for n in columns]
+        + [
             pltpu.VMEM((total, chunk, hidden), F32),
             pltpu.VMEM((total, chunk, 2 * hidden), BF16),
             pltpu.VMEM((total, chunk, width), F32),
@@ -480,6 +559,8 @@
             pltpu.VMEM((chunk, width), BF16),
             pltpu.VMEM((chunk, width), F32),
             pltpu.VMEM((chunk, width), BF16),
+            pltpu.SemaphoreType.DMA((6,)),
+            pltpu.SemaphoreType.DMA((len(columns), 2)),
             pltpu.SemaphoreType.DMA((total,)),
             pltpu.SemaphoreType.DMA((total,)),
             pltpu.SemaphoreType.DMA((total,)),
@@ -489,7 +570,7 @@
             collective_id=0, has_side_effects=True, vmem_limit_bytes=BLOCKS_VMEM
         ),
         name="blocks",
-    )(tokens, tokens, cotangent, cotangent, keep, perm, *weights)
+    )(tokens, cotangent, *large, *little)
 
 
 def local_grads(tokens, resets, cotangent, stacked):
@@ -499,12 +580,12 @@
     total = rows * (seq // chunk)
     span = chunk // LANES
     keep = (1 - resets).astype(F32).reshape(total, LANES, span)
-    keep = keep.transpose(0, 2, 1).reshape(total, chunk, 1)
-    keep = jnp.broadcast_to(keep, (total, chunk, 128))
-    at = lax.broadcasted_iota(jnp.int32, (chunk, chunk), 0)
-    source = lax.broadcasted_iota(jnp.int32, (chunk, chunk), 1)
-    perm = (source == (at % LANES) * span + at // LANES).astype(BF16)
-    perm_t = (at == (source % LANES) * span + source // LANES).astype(BF16)
+    keep = keep.transpose(0, 2, 1).reshape(total, chunk)
+    at = np.arange(chunk)
+    source = (at % LANES) * span + at // LANES
+    perm_t = np.equal(at[:, None], source[None, :])
+    perm = jnp.asarray(perm_t.T, BF16)
+    perm_t = jnp.asarray(perm_t, BF16)
     operands, active, low, *grads, grad_in, small = run_blocks(
         tokens, cotangent, keep, perm, weights, chunk
     )
@@ -973,6 +1054,7 @@
 
 def unpack_kernel(
     perm_t,
+    small_i,
     low_i,
     grad_i,
     down_i,
@@ -987,7 +1069,13 @@
     w_out,
     w_up,
     w_down,
+    *vectors,
 ):
+    at = 0
+    for vector in vectors:
+        n = vector.shape[1]
+        vector[...] = small_i[:, at : at + n]
+        at += n
     for source, target in (
         (down_i, w_down),
         (up_i, w_up),
@@ -997,16 +1085,12 @@
     ):
         target[0] = source[0].astype(F32)
     block_out[...] = dot(perm_t[...], low_i[0]).astype(BF16).reshape(block_out.shape)
-    grad = grad_i[0]
-    high = grad.astype(BF16)
-    rest = jnp.where(lax.axis_index("section") == 0, grad - high.astype(F32), 0.0)
-    grad_in[...] = (dot(perm_t[...], high) + dot(perm_t[...], rest.astype(BF16))).reshape(
-        grad_in.shape
-    )
-
-
-def unpack(packed, low, grad, perm_t, rows, width, hidden, ff):
+    grad_in[...] = dot(perm_t[...], grad_i[0]).reshape(grad_in.shape)
+
+
+def unpack(packed, small, low, grad, perm_t, rows, width, hidden, ff):
     packed = packed.reshape(4, ff, width)
+    vectors = (width, width, width, width, ff, 2 * hidden, hidden)
     parts, chunk = low.shape[0], low.shape[1]
     chunks = parts // rows
     seq = chunks * chunk
@@ -1029,9 +1113,11 @@
             jax.ShapeDtypeStruct((1, hidden, width), F32),
             jax.ShapeDtypeStruct((1, width, ff), F32),
             jax.ShapeDtypeStruct((1, ff, width), F32),
-        ],
+        ]
+        + [jax.ShapeDtypeStruct((1, n), F32) for n in vectors],
         in_specs=[
             whole(perm_t),
+            whole(small),
             pl.BlockSpec((1, chunk, width), lambda t: (t, 0, 0)),
             pl.BlockSpec((1, chunk, width), lambda t: (t, 0, 0)),
             pl.BlockSpec((1, tall, width), lambda t: (0, t, 0)),
@@ -1054,10 +1140,11 @@
             pl.BlockSpec((1, short, width), lambda t: (0, t, 0)),
             pl.BlockSpec((1, tall, width), column_block),
             pl.BlockSpec((1, tall, width), lambda t: (0, t, 0)),
-        ],
+        ]
+        + [pl.BlockSpec((1, n), lambda t: (0, 0)) for n in vectors],
         compiler_params=pltpu.CompilerParams(vmem_limit_bytes=VMEM_LIMIT),
         name="unpack",
-    )(perm_t, low, grad, packed, packed, packed, packed, packed)
+    )(perm_t, small, low, grad, packed, packed, packed, packed, packed)
 
 
 def sum_gradients(operands, small, hidden, ff):
@@ -1123,26 +1210,16 @@
     return packed, small_sum
 
 
-def split_small(small, width, hidden, ff):
-    sizes = (width, width, width, width, ff, 2 * hidden, hidden)
-    out = []
-    at = 0
-    for n in sizes:
-        out.append(small[:, at : at + n])
-        at += n
-    return out
-
-
 def body(tokens, resets, cotangent, *stacked):
     rows, _, width = tokens.shape
     hidden = stacked[3].shape[2]
     ff = stacked[8].shape[2]
     low, grad_in, perm_t, (*operands, small) = local_grads(tokens, resets, cotangent, stacked)
     packed, small_sum = sum_gradients(operands, small, hidden, ff)
-    block_out, grad_in, w_gate, w_cand, w_out, w_up, w_down = unpack(
-        packed, low, grad_in, perm_t, rows, width, hidden, ff
+    block_out, grad_in, w_gate, w_cand, w_out, w_up, w_down, *vectors = unpack(
+        packed, small_sum, low, grad_in, perm_t, rows, width, hidden, ff
     )
-    g_one, b_out, g_two, b_down, b_up, b_gate, b_cand = split_small(small_sum, width, hidden, ff)
+    g_one, b_out, g_two, b_down, b_up, b_gate, b_cand = vectors
     grads = (g_one, w_gate, b_gate, w_cand, b_cand, w_out, b_out, g_two, w_up, b_up, w_down, b_down)
     return (block_out, grad_in) + grads
 

time: 242 us -> 226 us (0.934)
  Pallas kernels: 233 us -> 223 us
  local copies, waits for them, and re-layouts: 5.47 us -> 0.9 us
    pallas_call x1, Pallas kernels: 118 us -> 108 us  [run_blocks(): pl.pallas_call(functools.partial(blocks_kernel, rows, chunks), out_shape=...]
    slice x3 -> x0, local copies, waits for them, and re-layouts: 3.87 us -> none  [split_small(): out.append(small[:, at:at + n])]
where the time goes in v4:
time: 226 us; the launch traced here: 225 us
  Pallas kernels  223 us (99%)
    pallas_call x1, Pallas kernels, run_blocks(): pl.pallas_call(functools.partial(blocks_kernel, rows, chunks), out_shape=...  108 us
    pallas_call x1, Pallas kernels, sum_gradients(): pl.pallas_call(functools.partial(sum_kernel, line, rounds), out_shape=[ja...  101 us
    pallas_call x1, Pallas kernels, unpack(): pl.pallas_call(unpack_kernel, grid=(parts,), out_shape=[jax.ShapeDtypeStr...  13.6 us

profile of v4, /device:TPU:0, one launch (start us, length us, event | category | flops | bytes accessed | tf_op | source)
XLA Modules:
  0.0 225.2 jit_solution(6941199788433177737)
XLA Ops:
  0.6 0.7 subtract_convert_fusion
  1.3 0.1 reshape.58
  1.4 0.1 copy.32
  1.5 0.7 reshape.59.keep_rows
  2.3 107.9 %blocks.1 = (bf16[8,256,2048]{2,1,0:T(8,128)(2,1)}, bf16[8,256,2048]{2,1,0:T(8,128)(2,1)}, bf16[8,256,512]{2,1,0:T(8,128)(2,1)}, bf16[8,256,512]{2,1,0:T(8,128)(...) custom-call(bf16[2,1024,512]{2,1,0:T(8,128)(2,1)} %tok.1, ...), custom_call_target="tpu_custom_call" | custom-call | tf_op jit(solution)/shard_map/blocks/pallas_call | solution.py:535
  110.2 101.1 %sum_gradients.1 = (bf16[4,2,1024,512]{3,2,1,0:T(8,128)(2,1)}, f32[1,7168]{1,0:T(1,128)}) custom-call(bf16[2048,2048]{1,0:T(8,128)(2,1)} %bitcast.19, bf16[2048,2048]{1,0:T(8,128)(2,1)} %bitcast.20, bf16[2048,512]{1,0:T(8,128)(2,1)} %bitcast.24, bf16[2048,2048]{1,0:T(8,128)(2,1)} %bitcast.21, bf16[2048,512]{1,0:T(8,128)(2,1)} %bitcast.25, ...), custom_call_target="tpu_custom_call" | custom-call | tf_op jit(solution)/shard_map/sum_gradients/pallas_call | solution.py:1164
  211.3 13.6 %unpack.1 = (bf16[1,2,1024,512]{3,2,1,0:T(8,128)(2,1)}, f32[1,2,1024,512]{3,2,1,0:T(8,128)}, f32[1,512,2048]{2,1,0:T(8,128)}, f32[1,512,1024]{2,1,0:T(8,128)}, f...) custom-call(bf16[256,256]{1,0:T(8,128)(2,1)} %constant.7.clone.perm_, ...), custom_call_target="tpu_custom_call" | custom-call | tf_op jit(solution)/shard_map/unpack/pallas_call | solution.py:1105

commit v5 on v4

--- a/solution.py
+++ b/solution.py
@@ -71,19 +71,30 @@
 class Step:
     def __init__(self, step, rows, chunks):
         first = lax.axis_index("section") == 0
-        phase = step // (chunks + 1)
-        self.at = step % (chunks + 1)
+        apart = 2 * chunks
+        joint = chunks + 1
+        middle = step - apart
+        final = middle >= (2 * rows - 2) * joint
+        phase = jnp.where(step < apart, 0, jnp.where(final, 2 * rows - 1, 1 + middle // joint))
+        alone = (step < apart) | final
+        at = jnp.where(step < apart, step, middle - (2 * rows - 2) * joint)
+        along = middle % joint
+        self.early = jnp.where(alone, at // 2, jnp.minimum(along, chunks - 1))
+        self.late = jnp.where(alone, at // 2, jnp.maximum(along - 1, 0))
+        self.begins = jnp.where(alone, at % 2 == 0, along < chunks)
+        self.ends = jnp.where(alone, at % 2 == 1, along > 0)
         self.forward = jnp.where(first, phase < rows, phase % 2 == 0)
+        self.backward = jnp.logical_not(self.forward)
         self.row = jnp.where(first, phase % rows, phase // 2)
         base = self.row * chunks
         last = chunks - 1
-        self.mixer = base + jnp.minimum(self.at, last)
-        self.feed = base + jnp.maximum(self.at - 1, 0)
-        self.back_feed = base + jnp.maximum(last - self.at, 0)
-        self.back_mixer = base + jnp.minimum(chunks - self.at, last)
+        self.mixer = base + self.early
+        self.feed = base + self.late
+        self.back_feed = base + last - self.early
+        self.back_mixer = base + last - self.late
         total = rows * chunks
         self.next_mixer = jnp.minimum(self.mixer + 1, total - 1)
-        later = jnp.minimum(base + self.at + 1, total - 1)
+        later = jnp.minimum(base + self.early + 1, total - 1)
         self.next_back = later // chunks * chunks + last - later % chunks
 
 
@@ -160,7 +171,7 @@
     ff = w_up.shape[1]
     span = chunk // LANES
     total = rows * chunks
-    steps = 2 * rows * (chunks + 1)
+    steps = 4 * chunks + (2 * rows - 2) * (chunks + 1)
     stages = (
         (operands_o, operands_all),
         (active_o, active_all),
@@ -227,42 +238,44 @@
             load_copy(3).wait()
             load_copy(4).wait()
 
-        @pl.when(step.forward & (step.at == 0))
+        starts = step.begins & (step.early == 0)
+
+        @pl.when(step.forward & starts)
         def _():
             carry[...] = jnp.zeros_like(carry)
 
-        @pl.when(jnp.logical_not(step.forward) & (step.at == 0))
+        @pl.when(step.backward & starts)
         def _():
             carry_back[...] = jnp.zeros_like(carry_back)
 
-        @pl.when(step.forward & (step.at < chunks) & (section == 0))
+        @pl.when(step.forward & step.begins & (section == 0))
         def _():
             inputs[step.mixer] = coming[...]
 
-        @pl.when(step.forward & (step.at < chunks) & (section == 1))
+        @pl.when(step.forward & step.begins & (section == 1))
         def _():
             chunk_copy(step.mixer).wait_recv()
 
-        @pl.when(jnp.logical_not(step.forward) & (step.at < chunks) & (section == 0))
+        @pl.when(step.backward & step.begins & (section == 0))
         def _():
             back_copy(step.back_feed).wait_recv()
             coming_back[...] = received[step.back_feed]
 
-        @pl.when(step.forward & (step.at < chunks) & (step.mixer >= 2))
+        @pl.when(step.forward & step.begins & (step.mixer >= 2))
         def _():
             stage_copy(0, step.mixer).wait()
 
-        @pl.when(step.forward & (step.at > 0) & (step.feed >= 2))
+        @pl.when(step.forward & step.ends & (step.feed >= 2))
         def _():
             for which in (1, 2):
                 stage_copy(which, step.feed).wait()
 
-        @pl.when(jnp.logical_not(step.forward) & (step.at < chunks) & (step.row * chunks + step.at >= 2))
+        @pl.when(step.backward & step.begins & (step.mixer >= 2))
         def _():
             for which in (3, 4, 5):
                 stage_copy(which, step.back_feed).wait()
 
-        @pl.when(jnp.logical_not(step.forward) & (step.at > 0) & (step.row * chunks + step.at >= 3))
+        @pl.when(step.backward & step.ends & (step.feed >= 2))
         def _():
             for which in (6, 7, 8):
                 stage_copy(which, step.back_mixer).wait()
@@ -422,63 +435,62 @@
             yield
             coming_back[...] = dot(perm[...], raw_chunk(step.next_back)).astype(BF16)
 
-        opening = step.at == 0
-        closing = step.at == chunks
-        between = jnp.logical_not(opening | closing)
-        backward = jnp.logical_not(step.forward)
-
-        @pl.when(step.forward & opening)
+        both = step.begins & step.ends
+        only_first = jnp.logical_not(step.ends)
+        only_second = jnp.logical_not(step.begins)
+
+        @pl.when(step.forward & only_first)
         def _():
             interleave(mixer(), reorder())
 
-        @pl.when(step.forward & between)
+        @pl.when(step.forward & both)
         def _():
             interleave(mixer(), feed(), reorder())
 
-        @pl.when(step.forward & closing)
+        @pl.when(step.forward & only_second)
         def _():
             interleave(feed())
 
-        @pl.when(backward & opening)
+        @pl.when(step.backward & only_first)
         def _():
             interleave(back_feed(), back_reorder())
 
-        @pl.when(backward & between)
+        @pl.when(step.backward & both)
         def _():
             interleave(back_feed(), back_mixer(), back_reorder())
 
-        @pl.when(backward & closing)
+        @pl.when(step.backward & only_second)
         def _():
             interleave(back_mixer())
 
-        @pl.when(step.forward & jnp.logical_not(closing))
+        @pl.when(step.forward & step.ends & (section == 0))
+        def _():
+            send[step.feed] = low_o[step.feed % 2]
+            chunk_copy(step.feed).start()
+
+        @pl.when(step.backward & step.ends & (section == 1))
+        def _():
+            send[step.back_mixer] = grad_o[step.back_mixer % 2]
+            back_copy(step.back_mixer).start()
+
+        @pl.when(step.forward & step.begins)
         def _():
             stage_copy(0, step.mixer).start()
 
-        @pl.when(step.forward & jnp.logical_not(opening))
+        @pl.when(step.forward & step.ends)
         def _():
             for which in (1, 2):
                 stage_copy(which, step.feed).start()
 
-        @pl.when(backward & jnp.logical_not(closing))
+        @pl.when(step.backward & step.begins)
         def _():
             for which in (3, 4, 5):
                 stage_copy(which, step.back_feed).start()
 
-        @pl.when(backward & jnp.logical_not(opening))
+        @pl.when(step.backward & step.ends)
         def _():
             for which in (6, 7, 8):
                 stage_copy(which, step.back_mixer).start()
-
-        @pl.when(step.forward & jnp.logical_not(opening) & (section == 0))
-        def _():
-            send[step.feed] = low_o[step.feed % 2]
-            chunk_copy(step.feed).start()
-
-        @pl.when(backward & jnp.logical_not(opening) & (section == 1))
-        def _():
-            send[step.back_mixer] = grad_o[step.back_mixer % 2]
-            back_copy(step.back_mixer).start()
 
     partner_barrier_signal(partner)
     pl.when(section == 0)(lambda: raw_copy(tok).start())
@@ -754,11 +766,11 @@
             sources[g][1], narrow.at[g % 2], narrow_sem.at[g % 2]
         )
 
-    def load(g):
-        narrow_copy(g).start()
-        for half in (away, core):
-            for t in range(2):
-                wide_copy(g, half, t).start()
+    def load(g, half):
+        if half is away:
+            narrow_copy(g).start()
+        for t in range(2):
+            wide_copy(g, half, t).start()
 
     def side_at(side):
         return pl.ds(pl.multiple_of(side * side_rows, side_rows), side_rows)
@@ -977,17 +989,19 @@
         else:
             small_out[...] = total
 
+    load(0, away)
     ones = turned.shape[1] - width
     for slot in range(2):
         turned[slot, width:] = jnp.ones((ones, turned.shape[2]), BF16)
     def tiles():
-        load(0)
         for g in range(groups):
-            if g + 1 < groups:
-                load(g + 1)
-            narrow_copy(g).wait()
-            turned[g % 2, :width] = narrow[g % 2].T
             for half in (away, core):
+                if half is away:
+                    load(g, core)
+                    narrow_copy(g).wait()
+                    turned[g % 2, :width] = narrow[g % 2].T
+                elif g + 1 < groups:
+                    load(g + 1, away)
                 for t in range(2):
                     wide_copy(g, half, t).wait()
                     left = turned[(g if g < 3 or t == 1 else 2) % 2]
@@ -1020,7 +1034,7 @@
             halves -= 1
         else:
             advance(chains[item])
-        if halves == 0 and at % 4 == 0 and small_at <= rounds:
+        if halves == 0 and at % 8 == 0 and small_at <= rounds:
             small_round(small_at)
             small_at += 1
     while small_at <= rounds:

time: 226 us -> 212 us (0.938)
  Pallas kernels: 223 us -> 210 us
    pallas_call x1, Pallas kernels: 101 us -> 94.2 us  [sum_gradients(): pl.pallas_call(functools.partial(sum_kernel, line, rounds), out_shape=[ja...]
    pallas_call x1, Pallas kernels: 108 us -> 102 us  [run_blocks(): pl.pallas_call(functools.partial(blocks_kernel, rows, chunks), out_shape=...]
where the time goes in v5:
time: 212 us
  Pallas kernels  210 us (99%)
    pallas_call x1, Pallas kernels, run_blocks(): pl.pallas_call(functools.partial(blocks_kernel, rows, chunks), out_shape=...  102 us
    pallas_call x1, Pallas kernels, sum_gradients(): pl.pallas_call(functools.partial(sum_kernel, line, rounds), out_shape=[ja...  94.2 us
    pallas_call x1, Pallas kernels, unpack(): pl.pallas_call(unpack_kernel, grid=(parts,), out_shape=[jax.ShapeDtypeStr...  13.6 us

profile of v5, /device:TPU:0, one launch (start us, length us, event | category | flops | bytes accessed | tf_op | source)
XLA Modules:
  0.0 212.0 jit_solution(17269496073701670871)
XLA Ops:
  0.6 0.7 subtract_convert_fusion
  1.3 0.1 reshape.58
  1.4 0.1 copy.32
  1.5 0.7 reshape.59.keep_rows
  2.3 101.7 %blocks.1 = (bf16[8,256,2048]{2,1,0:T(8,128)(2,1)}, bf16[8,256,2048]{2,1,0:T(8,128)(2,1)}, bf16[8,256,512]{2,1,0:T(8,128)(2,1)}, bf16[8,256,512]{2,1,0:T(8,128)(...) custom-call(bf16[2,1024,512]{2,1,0:T(8,128)(2,1)} %tok.1, ...), custom_call_target="tpu_custom_call" | custom-call | tf_op jit(solution)/shard_map/blocks/pallas_call | solution.py:547
  103.9 94.2 %sum_gradients.1 = (bf16[4,2,1024,512]{3,2,1,0:T(8,128)(2,1)}, f32[1,7168]{1,0:T(1,128)}) custom-call(bf16[2048,2048]{1,0:T(8,128)(2,1)} %bitcast.19, bf16[2048,2048]{1,0:T(8,128)(2,1)} %bitcast.20, bf16[2048,512]{1,0:T(8,128)(2,1)} %bitcast.24, bf16[2048,2048]{1,0:T(8,128)(2,1)} %bitcast.21, bf16[2048,512]{1,0:T(8,128)(2,1)} %bitcast.25, ...), custom_call_target="tpu_custom_call" | custom-call | tf_op jit(solution)/shard_map/sum_gradients/pallas_call | solution.py:1178
  198.2 13.6 %unpack.1 = (bf16[1,2,1024,512]{3,2,1,0:T(8,128)(2,1)}, f32[1,2,1024,512]{3,2,1,0:T(8,128)}, f32[1,512,2048]{2,1,0:T(8,128)}, f32[1,512,1024]{2,1,0:T(8,128)}, f...) custom-call(bf16[256,256]{1,0:T(8,128)(2,1)} %constant.7.clone.perm_, ...), custom_call_target="tpu_custom_call" | custom-call | tf_op jit(solution)/shard_map/unpack/pallas_call | solution.py:1119
